TPU v7x, 128 devices: a whole 4x4x4 slice. The times are simulated.
128 devices in a mesh: img: 8 (over y, core), ori: 16 (over x, z).
Axes of the slice: x: 4, y: 4, z: 4, core: 2. Of those that a mesh axis runs over, the one named last changes fastest.
Arguments:
- images: bfloat16 [8192, 12288], P(('img', 'ori')), may hold values from -34 to 34
- projections: bfloat16 [9216, 12288], P('ori'), may hold values from -0.6 to 0.6
- search: int32 [512, 4], P(('img', 'ori')), may hold values from 0 to 15, all different within a row; in each aligned block of 4 rows (0 to 3, 4 to 7, ...) at most 2 rows name the same one
Outputs:
- weighted: bfloat16 [9216, 12288], P('ori', 'img')
- loglik: float32 [8192], P(('img', 'ori'))
Inputs may be any that keep to these rules, and one draw needn't show every extreme that they name: `search`: each row names 4 different orientation blocks. In the 4 rows of one device no block is named by more than 2 rows, and some block is named by exactly 2 of them.
All inputs are finite; a program needn't handle non-finite values.
Results may differ from a plain program's by a relative error of at most 0.01.
Values may be sent and summed in bfloat16 or wider, within the bound.
A program may use at most 128 MiB of HBM per device.

v0:
```python
import jax
import jax.numpy as jnp
from jax import lax
from jax.sharding import PartitionSpec as P


def per_device(images, projections, search):
    ori_count = lax.axis_size("ori")
    groups_dev = search.shape[0]
    per_group = search.shape[1]
    columns = images.shape[1]
    group_size = images.shape[0] // groups_dev
    ori_dev = projections.shape[0]
    capacity = max(2, 2 * groups_dev * per_group // ori_count)
    slot_count = ori_count * capacity
    entries = search.reshape(-1)
    onehot = (entries[:, None] == jnp.arange(ori_count, dtype=jnp.int32)[None, :]).astype(jnp.int32)
    before = jnp.cumsum(onehot, axis=0) - onehot
    ranking = jnp.sum(before * onehot, axis=1)
    slot_of = entries * capacity + ranking
    owner_group = jnp.arange(groups_dev * per_group, dtype=jnp.int32) // per_group
    matches = (slot_of[None, :] == jnp.arange(slot_count, dtype=jnp.int32)[:, None]).astype(
        jnp.int32
    )
    in_use = jnp.sum(matches, axis=1)
    source = jnp.sum(matches * owner_group[None, :], axis=1)
    grouped = images.reshape(groups_dev, group_size, columns)
    outgoing = grouped[source] * in_use.astype(jnp.bfloat16)[:, None, None]
    outgoing = outgoing.reshape(ori_count, capacity, group_size, columns)
    live_marks = jnp.broadcast_to(in_use.astype(jnp.bfloat16)[:, None], (slot_count, group_size))
    live_marks = live_marks.reshape(ori_count, capacity, group_size)
    half_norm = 0.5 * jnp.sum(jnp.square(projections.astype(jnp.float32)), axis=1)
    arrived_images = lax.all_to_all(outgoing, "ori", split_axis=0, concat_axis=0, tiled=True)
    arrived_marks = lax.all_to_all(live_marks, "ori", split_axis=0, concat_axis=0, tiled=True)
    scores = (
        jnp.einsum("sigk,jk->sigj", arrived_images, projections, preferred_element_type=jnp.float32)
        - half_norm
    )
    arrived, arrived_marks, scores = (arrived_images, arrived_marks, scores)
    slot_rows = ori_count * capacity * group_size
    scores = scores.reshape(ori_count, capacity * group_size, ori_dev)
    local_max = jnp.max(scores, axis=2)
    local_sum = jnp.sum(jnp.exp(scores - local_max[..., None]), axis=2)
    back_max, back_sum = (
        lax.all_to_all(local_max, "ori", split_axis=0, concat_axis=0, tiled=True),
        lax.all_to_all(local_sum, "ori", split_axis=0, concat_axis=0, tiled=True),
    )
    entry_max = back_max.reshape(slot_count, group_size)[slot_of].reshape(
        groups_dev, per_group, group_size
    )
    entry_sum = back_sum.reshape(slot_count, group_size)[slot_of].reshape(
        groups_dev, per_group, group_size
    )
    highest = jnp.max(entry_max, axis=1)
    loglik = highest + jnp.log(
        jnp.sum(jnp.exp(entry_max - highest[:, None, :]) * entry_sum, axis=1)
    )
    norm_slots = loglik[source] * in_use.astype(jnp.float32)[:, None]
    norm_slots = norm_slots.reshape(ori_count, capacity * group_size)
    arrived_lse = lax.all_to_all(norm_slots, "ori", split_axis=0, concat_axis=0, tiled=True)
    live_float = arrived_marks.reshape(ori_count, capacity * group_size).astype(jnp.float32)
    responsibility = (jnp.exp(scores - arrived_lse[..., None]) * live_float[..., None]).astype(
        jnp.bfloat16
    )
    responsibility = responsibility.reshape(slot_rows, ori_dev)
    flat_images = arrived.reshape(slot_rows, columns)
    partial_sum = lax.dot_general(
        responsibility, flat_images, (((0,), (0,)), ((), ())), preferred_element_type=jnp.float32
    )
    summed = lax.psum_scatter(partial_sum, "img", scatter_dimension=1, tiled=True)
    return (summed.astype(jnp.bfloat16), loglik.reshape(-1))


def solution(mesh):
    placed = (P(("img", "ori"), None), P("ori", None), P(("img", "ori"), None))
    return jax.shard_map(
        per_device,
        mesh=mesh,
        in_specs=placed,
        out_specs=(P("ori", "img"), P(("img", "ori"))),
        check_vma=False,
    )
```

profile of v0, /device:TPU:1, one launch (start us, length us, event | category | flops | bytes accessed | tf_op | source)
XLA Modules:
  0.0 493.1 jit_solution(3609634691040103917)
XLA Ops:
  7.2 0.9 reshape.183
  8.6 6.5 %gather_fusion = bf16[32,16,12288]{2,1,0:T(8,128)(2,1)} fusion(bf16[4,16,12288]{2,1,0:T(8,128)(2,1)S(1)} %bitcast.30, s32[1024]{0:T(1024)S(1)} %pad_clamp_fusion.1), kind=kCustom, calls=%fused_computation | custom fusion | bytes 25165952 | tf_op jit(solution)/shard_map/gather | solution.py:28
  15.1 10.6 %broadcast_multiply_fusion = bf16[16,2,16,12288]{3,2,1,0:T(8,128)(2,1)} fusion(bf16[16,2,16,12288]{3,2,1,0:T(8,128)(2,1)} %bitcast.31, bf16[16,2]{1,0:T(8,128)(2,1)S(1)} %convert_element_type.52), kind=kLoop, calls=%fused_computation.8 | loop fusion | flops 6291456 | bytes 25165888 | tf_op jit(solution)/shard_map/mul | solution.py:28
  25.7 8.6 %all-to-all-start = ((bf16[16,2,16,12288]{3,2,1,0:T(8,128)(2,1)}), bf16[16,2,16,12288]{3,2,1,0:T(8,128)(2,1)}, u32[]{:S(2)}, u32[]{:S(2)}) async-start(bf16[16,2,16,12288]{3,2,1,0:T(8,128)(2,1)} %broadcast_multiply_fusion), calls=%async_computation | async-start | bytes 25165824 | tf_op jit(solution)/shard_map/all_to_all | solution.py:33
  34.4 7.9 %multiply_reduce_fusion = f32[576]{0:T(1024)S(1)} fusion(bf16[576,12288]{1,0:T(8,128)(2,1)} %param.4), kind=kLoop, calls=%fused_computation.4 | loop fusion | flops 21233088 | bytes 14158080 | tf_op jit(solution)/shard_map/reduce_sum | solution.py:32
  42.3 207.8 %all-to-all-done = bf16[16,2,16,12288]{3,2,1,0:T(8,128)(2,1)} async-done(((bf16[16,2,16,12288]{3,2,1,0:T(8,128)(2,1)}), bf16[16,2,16,12288]{3,2,1,0:T(8,128)(2,1)}, u32[]{:S(2)}, u32[]{:S(2)}) %all-to-all-start) | async-done | bytes 12582944 | tf_op jit(solution)/shard_map/all_to_all | solution.py:33
  250.1 15.2 %fusion.11 = (f32[16,2,16]{2,1,0:T(2,128)S(1)}, f32[16,2,16,576]{3,2,1,0:T(8,128)S(1)}) fusion(f32[576]{0:T(1024)S(1)} %broadcast_multiply_fusion.1, bf16[16,2,16,12288]{3,2,1,0:T(8,128)(2,1)} %all-to-all-done, bf16[576,12288]{1,0:T(8,128)(2,1)} %param.4), kind=kOutput, calls=%fused_computation.37 | convolution fusion | flops 7248346624 | bytes 27922688 | tf_op jit(solution)/shard_map/sigk,jk->sigj/dot_general | solution.py:36
  265.3 0.4 exponential_reduce_fusion
  265.7 0.7 all_to_all.25
  266.4 13.4 %all-to-all-start.2 = ((f32[16,1,32]{2,1,0:T(1,128)}), f32[16,1,32]{2,1,0:T(1,128)S(1)}, u32[]{:S(2)}, u32[]{:S(2)}) async-start(f32[16,1,32]{2,1,0:T(1,128)} %all_to_all.25), calls=%async_computation.2 | async-start | bytes 16384 | tf_op jit(solution)/shard_map/all_to_all | solution.py:46
  279.8 0.7 all_to_all.23
  280.5 5.7 %all-to-all-done.2 = f32[16,1,32]{2,1,0:T(1,128)S(1)} async-done(((f32[16,1,32]{2,1,0:T(1,128)}), f32[16,1,32]{2,1,0:T(1,128)S(1)}, u32[]{:S(2)}, u32[]{:S(2)}) %all-to-all-start.2) | async-done | bytes 2080 | tf_op jit(solution)/shard_map/all_to_all | solution.py:46
  286.2 3.5 all-to-all-start.1
  289.9 0.5 broadcast.149
  290.4 0.7 reduce.12
  291.2 4.7 all-to-all-done.1
  295.9 0.7 broadcast_in_dim.2
  296.6 3.5 all-to-all-start.4
  300.1 0.7 reduce.11
  300.8 0.6 gather_fusion.2
  301.4 0.6 gather_fusion.1
  302.0 0.6 gather_fusion.3
  302.7 0.6 mul.93
  303.3 3.1 all-to-all-done.4
  306.4 3.5 all-to-all-start.3
  309.9 0.2 reduce-scatter.2.cloned.1.call-start
  310.1 6.2 %all-to-all-done.3 = f32[16,1,32]{2,1,0:T(1,128)S(1)} async-done(((f32[16,1,32]{2,1,0:T(1,128)}), f32[16,1,32]{2,1,0:T(1,128)S(1)}, u32[]{:S(2)}, u32[]{:S(2)}) %all-to-all-start.3) | async-done | bytes 2080 | tf_op jit(solution)/shard_map/all_to_all | solution.py:60
  316.3 0.7 reduce.13
  317.1 16.1 %convolution_bitcast_fusion = f32[576,12288]{1,0:T(8,128)} fusion(bf16[16,2,16,12288]{3,2,1,0:T(8,128)(2,1)} %all-to-all-done, f32[16,2,16,576]{3,2,1,0:T(8,128)S(1)} %get-tuple-element.7, f32[16,2,16]{2,1,0:T(2,128)S(1)} %convert_element_type.56, f32[16,2,16]{2,1,0:T(2,128)S(1)} %sub.52), kind=kOutput, calls=%fused_computation.5 | convolution fusion | flops 7248642048 | bytes 42078208 | tf_op jit(solution)/shard_map/dot_general | solution.py:67
  333.1 0.6 add.57
  333.7 149.1 %reduce-scatter.2.cloned.1.call-done = f32[576,1536]{1,0:T(8,128)} async-done(((f32[576,12288]{1,0:T(8,128)}), f32[576,1536]{1,0:T(8,128)}) %reduce-scatter.2.cloned.1.call-update) | async-done | bytes 3538960 | tf_op jit(solution)/shard_map/reduce_scatter | solution.py:70
  482.8 3.4 convert_element_type.58
  (32 shorter events, 1.3 us)
Async XLA Ops:
  7.2 1.4 copy-start
  25.7 8.6 %copy-start.2 = (s32[4,4]{1,0:T(4,128)S(1)}, s32[4,4]{1,0:T(4,128)}, u32[]{:S(2)}) copy-start(s32[4,4]{1,0:T(4,128)} %param.5) | copy-start | bytes 196
  25.7 224.3 %all-to-all-start = ((bf16[16,2,16,12288]{3,2,1,0:T(8,128)(2,1)}), bf16[16,2,16,12288]{3,2,1,0:T(8,128)(2,1)}, u32[]{:S(2)}, u32[]{:S(2)}) async-start(bf16[16,2,16,12288]{3,2,1,0:T(8,128)(2,1)} %broadcast_multiply_fusion), calls=%async_computation | async-start | bytes 25165824 | tf_op jit(solution)/shard_map/all_to_all | solution.py:33
  266.4 19.8 %all-to-all-start.2 = ((f32[16,1,32]{2,1,0:T(1,128)}), f32[16,1,32]{2,1,0:T(1,128)S(1)}, u32[]{:S(2)}, u32[]{:S(2)}) async-start(f32[16,1,32]{2,1,0:T(1,128)} %all_to_all.25), calls=%async_computation.2 | async-start | bytes 16384 | tf_op jit(solution)/shard_map/all_to_all | solution.py:46
  286.2 9.8 %all-to-all-start.1 = ((f32[16,1,32]{2,1,0:T(1,128)}), f32[16,1,32]{2,1,0:T(1,128)S(1)}, u32[]{:S(2)}, u32[]{:S(2)}) async-start(f32[16,1,32]{2,1,0:T(1,128)} %all_to_all.23), calls=%async_computation.1 | async-start | bytes 16384 | tf_op jit(solution)/shard_map/all_to_all | solution.py:45
  296.6 9.8 %all-to-all-start.4 = ((bf16[16,2,16]{2,1,0:T(2,128)(2,1)}), bf16[16,2,16]{2,1,0:T(2,128)(2,1)S(1)}, u32[]{:S(2)}, u32[]{:S(2)}) async-start(bf16[16,2,16]{2,1,0:T(2,128)(2,1)} %broadcast_in_dim.2), calls=%async_computation.4 | async-start | bytes 16384 | tf_op jit(solution)/shard_map/all_to_all | solution.py:34
  306.4 9.9 %all-to-all-start.3 = ((f32[16,1,32]{2,1,0:T(1,128)}), f32[16,1,32]{2,1,0:T(1,128)S(1)}, u32[]{:S(2)}, u32[]{:S(2)}) async-start(f32[16,1,32]{2,1,0:T(1,128)} %bitcast.10), calls=%async_computation.3 | async-start | bytes 16384 | tf_op jit(solution)/shard_map/all_to_all | solution.py:60
  309.9 172.9 %reduce-scatter.2.cloned.1.call-start = ((), (), s32[]{:S(2)}) async-start(), calls=%async_computation.6 | async-start | bytes 31850496 | tf_op jit(solution)/shard_map/reduce_scatter | solution.py:70
  333.1 153.1 %copy-start.1 = (bf16[64,12288]{1,0:T(8,128)(2,1)S(1)}, bf16[64,12288]{1,0:T(8,128)(2,1)}, u32[]{:S(2)}) copy-start(bf16[64,12288]{1,0:T(8,128)(2,1)} %param.3) | copy-start | bytes 4718596
Sparse Core Ops, SparseCore 0:
  333.3 149.4 reduce-scatter.1
where the time goes:
time: 494 us; the launch traced here: 493 us
  waiting for transfers between devices  377 us (76%)
  starting transfers between devices  32.6 us (7%)
  matrix products  31.2 us (6%)
  other arithmetic  25.4 us (5%)
  between operations  14.2 us (3%)
  local copies, waits for them, and re-layouts  13 us (3%)
    all_to_all x1, waiting for transfers between devices, per_device(): lax.all_to_all(outgoing, 'ori', split_axis=0, concat_axis=0, tiled=True)  208 us
    reduce_scatter x1, waiting for transfers between devices, per_device(): lax.psum_scatter(partial_sum, 'img', scatter_dimension=1, tiled=True)  149 us
    dot_general x1, matrix products, per_device(): lax.dot_general(responsibility, flat_images, (((0,), (0,)), ((), ())), pr...  16.1 us
    dot_general x1, matrix products, per_device(): jnp.einsum('sigk,jk->sigj', arrived_images, projections, preferred_elemen...  15.2 us
    all_to_all x1, starting transfers between devices, per_device(): lax.all_to_all(local_sum, 'ori', split_axis=0, concat_axis=0, tiled=True)  13.4 us
    mul x1, other arithmetic, per_device(): outgoing = grouped[source] * in_use.astype(jnp.bfloat16)[:, None, None]  10.6 us
  transfers between devices with their start and end apart: 6, of which 6 were waited for; matrix products, arithmetic and copies ran while one was open for 3% of the time, Pallas kernels for 0%

commit v1 on v0

v1 whole, which is shorter than its diff:
```python
import functools
import math

import jax
import jax.numpy as jnp
from jax import lax
from jax.experimental import pallas as pl
from jax.experimental.pallas import tpu as pltpu
from jax.sharding import PartitionSpec as P

MESH = pl.DeviceIdType.MESH
SIDE = 4
CORES = 2
SLOTS = 2
LANES = 128
NO_SCORE = -3.0e38


def ring(position, step):
    return lax.rem(position + step + SIDE, SIDE)


def coordinates():
    m, b = lax.axis_index("img"), lax.axis_index("ori")
    return lax.div(m, CORES), lax.rem(m, CORES), lax.div(b, SIDE), lax.rem(b, SIDE)


def at_img(y, c):
    return {"img": y * CORES + c, "ori": lax.axis_index("ori")}


def at_ori(x, z):
    return {"img": lax.axis_index("img"), "ori": x * SIDE + z}


def remote(source, target, send, recv, device):
    return pltpu.make_async_remote_copy(
        src_ref=source,
        dst_ref=target,
        send_sem=send,
        recv_sem=recv,
        device_id=device,
        device_id_type=MESH,
    )


def greet(devices):
    barrier = pltpu.get_barrier_semaphore()
    for device in devices:
        pl.semaphore_signal(barrier, inc=1, device_id=device, device_id_type=MESH)
    pl.semaphore_wait(barrier, len(devices))


TURNS = [(0, 0), (0, 1), (1, 0), (1, 1), (3, 0), (3, 1), (2, 0), (2, 1)]


def slot_table(search):
    blocks = SIDE * SIDE
    lane = lax.broadcasted_iota(jnp.int32, (8, LANES), 1)
    b, s = lax.rem(lane, blocks), lax.div(lane, blocks)
    table = jnp.full((8, LANES), -1.0, jnp.float32)
    rank = jnp.zeros((8, LANES), jnp.int32)
    for g in range(search.shape[0]):
        hit = b == search[g, 0]
        for n in range(1, search.shape[1]):
            hit = hit | (b == search[g, n])
        table = jnp.where(hit & (rank == s), float(g), table)
        rank = rank + hit.astype(jnp.int32)
    return table


def spread_kernel(
    search,
    images,
    xa,
    xb,
    tables,
    told,
    home_sem,
    turn_send,
    turn_recv,
    near_send,
    near_recv,
    far_send,
    far_recv,
    told_send,
    told_recv,
    table_send,
    table_recv,
):
    y, c, x, z = coordinates()
    rows, half = xa.shape[2], xa.shape[3]
    mid = rows // 2
    me = y * CORES + c
    img_peers = [at_img(ring(y, dy), lax.rem(c + dc, CORES)) for dy, dc in TURNS[1:]]
    steps = [(dx, dz) for dx in range(SIDE) for dz in range(SIDE) if (dx, dz) != (0, 0)]
    plane = [at_ori(ring(x, dx), ring(z, dz)) for dx, dz in steps]
    ori_peers = [at_ori(ring(x, 1), z), at_ori(ring(x, -1), z), at_ori(x, ring(z, 1)), at_ori(x, ring(z, -1))]
    greet(img_peers + plane)

    def columns(m, part):
        return images.at[:, pl.ds(pl.multiple_of(m * (2 * half) + part * half, 128), half)]

    turned, home = [], []
    for k, (dy, dc) in enumerate(TURNS):
        to_y, to_c = ring(y, dy), lax.rem(c + dc, CORES)
        to_m = to_y * CORES + to_c
        for part, (line, place) in enumerate(((xa, x), (xb, z))):
            if k == 0:
                copy = pltpu.make_async_copy(columns(to_m, part), line.at[place, me], home_sem.at[part])
                home.append(copy)
            else:
                copy = remote(
                    columns(to_m, part), line.at[place, me], turn_send.at[k, part], turn_recv.at[k, part], at_img(to_y, to_c)
                )
                turned.append(copy)
            copy.start()
    told[me] = slot_table(search)
    tells = [
        remote(told.at[me], told.at[me], told_send.at[k], told_recv.at[k], peer) for k, peer in enumerate(img_peers)
    ]
    for copy in tells:
        copy.start()

    near = {}
    far = []

    def start_near(k):
        dy, dc = TURNS[k]
        source = ring(y, -dy) * CORES + lax.rem(c + dc, CORES)
        for way in range(4):
            line, place = (xa, x) if way < 2 else (xb, z)
            block = line.at[place, source]
            near[k, way] = remote(block, block, near_send.at[k, way], near_recv.at[k, way], ori_peers[way])
            near[k, way].start()

    def start_far(k):
        dy, dc = TURNS[k]
        source = ring(y, -dy) * CORES + lax.rem(c + dc, CORES)
        for way in range(4):
            line, place = (xa, x) if way < 2 else (xb, z)
            forward = way % 2 == 0
            near[k, way].wait_recv()
            block = line.at[ring(place, -1 if forward else 1), source, pl.ds(0 if forward else mid, mid)]
            copy = remote(block, block, far_send.at[k, way], far_recv.at[k, way], ori_peers[way])
            copy.start()
            far.append(copy)

    for k in range(len(TURNS)):
        for part in range(2):
            if k == 0:
                home[part].wait()
            else:
                turned[2 * (k - 1) + part].wait_recv()
        start_near(k)
        if k > 0:
            start_far(k - 1)
    for copy in tells:
        copy.wait_recv()
    b = x * SIDE + z
    sublane = lax.broadcasted_iota(jnp.int32, (8, LANES), 0)
    gathered = told[0]
    for m in range(1, told.shape[0]):
        gathered = jnp.where(sublane == m, told[m], gathered)
    tables[b] = gathered
    spreads = [
        remote(tables.at[b], tables.at[b], table_send.at[k], table_recv.at[k], peer) for k, peer in enumerate(plane)
    ]
    for copy in spreads:
        copy.start()
    start_far(len(TURNS) - 1)
    for copy in tells:
        copy.wait_send()
    for copy in spreads:
        copy.wait()
    for copy in turned + list(near.values()):
        copy.wait_send()
    for copy in far:
        copy.wait()


def spread(search, images):
    rows, columns = images.shape
    blocks = SIDE * SIDE
    planes = SIDE * CORES
    half = columns // planes // 2
    line = jax.ShapeDtypeStruct((SIDE, planes, rows, half), images.dtype)
    turns = len(TURNS)
    return pl.pallas_call(
        spread_kernel,
        out_shape=(line, line, jax.ShapeDtypeStruct((blocks, planes, LANES), jnp.float32)),
        in_specs=[pl.BlockSpec(memory_space=pltpu.SMEM), pl.BlockSpec(memory_space=pl.ANY)],
        out_specs=(
            pl.BlockSpec(memory_space=pl.ANY),
            pl.BlockSpec(memory_space=pl.ANY),
            pl.BlockSpec(memory_space=pltpu.VMEM),
        ),
        scratch_shapes=[
            pltpu.VMEM((planes, 8, LANES), jnp.float32),
            pltpu.SemaphoreType.DMA((2,)),
            pltpu.SemaphoreType.DMA((turns, 2)),
            pltpu.SemaphoreType.DMA((turns, 2)),
            pltpu.SemaphoreType.DMA((turns, 4)),
            pltpu.SemaphoreType.DMA((turns, 4)),
            pltpu.SemaphoreType.DMA((turns, 4)),
            pltpu.SemaphoreType.DMA((turns, 4)),
            pltpu.SemaphoreType.DMA((planes - 1,)),
            pltpu.SemaphoreType.DMA((planes - 1,)),
            pltpu.SemaphoreType.DMA((blocks - 1,)),
            pltpu.SemaphoreType.DMA((blocks - 1,)),
        ],
        compiler_params=pltpu.CompilerParams(collective_id=0, has_side_effects=True),
        cost_estimate=pl.CostEstimate(flops=0, bytes_accessed=16 * 2**20, transcendentals=0),
    )(search, images)


ROUNDS = [2, 1, 3, 0]


def main_kernel(
    tables,
    xa_hbm,
    xb_hbm,
    projections,
    weighted,
    loglik,
    xa,
    xb,
    proj,
    picks,
    arrived,
    out_a,
    out_b,
    pair_out,
    pair_in,
    kept,
    y_in,
    stats,
    resp,
    total,
    load_sem,
    a_send,
    a_recv,
    b_send,
    b_recv,
    pair_send,
    pair_recv,
    y_send,
    y_recv,
    stat_send,
    stat_recv,
    r_send,
    r_recv,
    rc_send,
    rc_recv,
):
    y, c, x, z = coordinates()
    me = y * CORES + c
    block = x * SIDE + z
    blocks = SIDE * SIDE
    other = 1 - c
    group, half = arrived.shape[5], arrived.shape[6] // 2
    slice_columns = 2 * half
    oris = proj.shape[0]
    lanes = kept.shape[2]

    loads = [
        pltpu.make_async_copy(xa_hbm, xa, load_sem.at[0]),
        pltpu.make_async_copy(xb_hbm, xb, load_sem.at[1]),
        pltpu.make_async_copy(
            projections.at[:, pl.ds(pl.multiple_of(me * slice_columns, 128), slice_columns)], proj, load_sem.at[2]
        ),
    ]
    for copy in loads:
        copy.start()
    ori_peers = [
        (dx, dz, at_ori(ring(x, dx), ring(z, dz))) for dx in range(SIDE) for dz in range(SIDE) if (dx, dz) != (0, 0)
    ]
    partner = at_img(y, other)
    y_peers = [at_img(ring(y, d), c) for d in range(1, SIDE)]
    greet([device for _, _, device in ori_peers] + [partner] + y_peers)
    loads[0].wait()
    loads[1].wait()

    planes = xa.shape[1]
    lane_row = lax.broadcasted_iota(jnp.int32, (LANES, LANES), 0)
    for d in range(SIDE):
        for s in range(SLOTS):
            for part, dest in enumerate((x * SIDE + ring(z, d), ring(x, d) * SIDE + z)):
                column = jnp.where(lane_row == s * blocks + dest, 1.0, 0.0)
                for p in range(SIDE):
                    home = p * SIDE + z if part == 0 else x * SIDE + p
                    picks[part, d, s, p] = jnp.dot(tables[home], column, preferred_element_type=jnp.float32)

    def fill(j):
        home_y = ring(y, ROUNDS[j])
        slot = j % 2

        def step(n, carry):
            cc, p = lax.div(n, SIDE), lax.rem(n, SIDE)
            m = home_y * CORES + cc
            for part, line in enumerate((xa, xb)):
                choices = [line[p, m, g * group : (g + 1) * group, :] for g in range(line.shape[2] // group)]
                for d in range(SIDE):
                    for s in range(SLOTS):
                        pick = jnp.broadcast_to(picks[part, d, s, p, pl.ds(m, 1), :], (group, LANES))
                        pick = jnp.concatenate([pick.astype(jnp.bfloat16)] * (half // LANES), axis=1)
                        value = choices[0]
                        for g in range(1, len(choices)):
                            value = jnp.where(pick == g, choices[g], value)
                        if d and part == 0:
                            out_a[slot, d - 1, cc, s, p] = value
                        elif d:
                            out_b[slot, d - 1, cc, s, p] = value
                        elif part == 0:
                            arrived[j, cc, s, z, p, :, 0:half] = value
                        else:
                            arrived[j, cc, s, p, x, :, half : 2 * half] = value
            return carry

        lax.fori_loop(0, CORES * SIDE, step, 0)

    moves = {}

    def send(j):
        slot = j % 2
        moves[j] = []
        for d in (2, 1, 3):
            moves[j].append(
                remote(
                    out_a.at[slot, d - 1],
                    arrived.at[j, :, :, z, :, :, pl.ds(0, half)],
                    a_send.at[slot, d - 1],
                    a_recv.at[j, d - 1],
                    at_ori(x, ring(z, d)),
                )
            )
            moves[j].append(
                remote(
                    out_b.at[slot, d - 1],
                    arrived.at[j, :, :, :, x, :, pl.ds(half, half)],
                    b_send.at[slot, d - 1],
                    b_recv.at[j, d - 1],
                    at_ori(ring(x, d), z),
                )
            )
        for copy in moves[j]:
            copy.start()

    fill(0)
    send(0)
    fill(1)
    send(1)
    loads[2].wait()
    wide = proj[...].astype(jnp.float32)
    half_norm = 0.5 * jnp.sum(wide * wide, axis=1, keepdims=True)

    def scores(j, cc):
        rows = arrived[j, cc].reshape(lanes, slice_columns)
        return (
            lax.dot_general(proj[...], rows, (((1,), (1,)), ((), ())), preferred_element_type=jnp.float32) - half_norm
        )

    pairs, sums = [], []
    for j in range(SIDE):
        for copy in moves[j]:
            copy.wait_recv()
        if j + 2 < SIDE:
            for copy in moves[j]:
                copy.wait_send()
            fill(j + 2)
            send(j + 2)
        slot = j % 2
        if j >= 2:
            pairs[j - 2].wait_send()
        pair_out[slot] = scores(j, other)
        copy = remote(pair_out.at[slot], pair_in.at[j], pair_send.at[slot], pair_recv.at[j], partner)
        copy.start()
        pairs.append(copy)
        kept[j] = scores(j, c)
        copy.wait_recv()
        kept[j] += pair_in[j]
        d = ROUNDS[j]
        if d:
            copy = remote(kept.at[j], y_in.at[d - 1], y_send.at[d - 1], y_recv.at[d - 1], y_peers[d - 1])
            copy.start()
            sums.append(copy)
    for j in (2, 3):
        for copy in moves[j]:
            copy.wait_send()
        pairs[j].wait_send()
    for copy in sums:
        copy.wait()

    last = SIDE - 1
    kept[last] = kept[last] + y_in[0] + y_in[1] + y_in[2]
    highest = jnp.max(kept[last], axis=0, keepdims=True)
    weight = jnp.sum(jnp.exp(kept[last] - highest), axis=0, keepdims=True)
    which = lax.broadcasted_iota(jnp.int32, (8, lanes), 0)
    stats[block] = jnp.where(which == 0, highest, weight)
    told = []
    for dx, dz, device in ori_peers:
        k = dx * SIDE + dz
        told.append(remote(stats.at[block], stats.at[block], stat_send.at[k], stat_recv.at[k], device))
        told[-1].start()
    for copy in told:
        copy.wait()

    tops, masses = stats[:, 0, :], stats[:, 1, :]
    images = lanes // SLOTS
    home_row = lax.broadcasted_iota(jnp.int32, (blocks, images), 0)
    home_lane = lax.div(lax.broadcasted_iota(jnp.int32, (blocks, images), 1), group)
    spot = lax.rem(home_lane, SIDE) * SIDE + lax.div(home_lane, SIDE)
    widen = jnp.where(home_row == spot, 1.0, 0.0)
    plane = tables[:, pl.ds(me, 1), :].reshape(blocks, LANES)
    named = lax.dot_general(plane, widen, (((0,), (0,)), ((), ())), preferred_element_type=jnp.float32)
    named = jnp.concatenate([named[s * blocks : (s + 1) * blocks] for s in range(SLOTS)], axis=1)
    block_row = lax.broadcasted_iota(jnp.int32, (blocks, lanes), 0)
    own = jnp.sum(jnp.where(block_row == block, named, 0.0), axis=0, keepdims=True)
    norm = jnp.zeros((1, lanes), jnp.float32)
    for g in range(loglik.shape[0]):
        listed = named == g
        top = jnp.max(jnp.where(listed, tops, NO_SCORE), axis=0, keepdims=True)
        top = jnp.maximum(top[:, :images], top[:, images:])
        top2 = jnp.concatenate([top, top], axis=1)
        mass = jnp.where(listed, jnp.exp(jnp.minimum(tops - top2, 0.0)) * masses, 0.0)
        mass = jnp.sum(mass, axis=0, keepdims=True)
        value = top + jnp.log(mass[:, :images] + mass[:, images:])
        loglik[pl.ds(g, 1), :] = value
        norm = jnp.where(own == g, jnp.concatenate([value, value], axis=1), norm)
    resp[0, c] = jnp.where(own >= 0, jnp.exp(kept[last] - norm), 0.0).astype(jnp.bfloat16)

    sent, crossed = {}, {}
    for d in (2, 1, 3):
        sent[d] = remote(resp.at[0, c], resp.at[d, c], r_send.at[d], r_recv.at[d], at_img(ring(y, -d), c))
        sent[d].start()
    crossed[0] = remote(resp.at[0, c], resp.at[0, c], rc_send.at[0], rc_recv.at[0], partner)
    crossed[0].start()

    tile = 512

    def add(d, cc, first=False, final=False):
        j = ROUNDS.index(d)
        for t in range(slice_columns // tile):
            cols = slice(t * tile, (t + 1) * tile)
            rows = arrived[j, cc, :, :, :, :, cols].reshape(lanes, tile)
            part = jnp.dot(resp[d, cc], rows, preferred_element_type=jnp.float32)
            if not first:
                part = part + total[:, cols]
            if final:
                weighted[:, cols] = part.astype(weighted.dtype)
            else:
                total[:, cols] = part

    add(0, c, first=True)
    crossed[0].wait_recv()
    add(0, other)
    for d in (1, 3, 2):
        sent[d].wait_recv()
        crossed[d] = remote(resp.at[d, c], resp.at[d, c], rc_send.at[d], rc_recv.at[d], partner)
        crossed[d].start()
        add(d, c)
        crossed[d].wait_recv()
        add(d, other, final=d == 2)
    for d in range(SIDE):
        if d:
            sent[d].wait_send()
        crossed[d].wait_send()


def per_device(images, projections, search):
    blocks = SIDE * SIDE
    groups, _ = search.shape
    rows, columns = images.shape
    planes = SIDE * CORES
    group = rows // groups
    slice_columns = columns // planes
    half = slice_columns // 2
    oris = projections.shape[0]
    lanes = blocks * SLOTS * group
    images_plane = blocks * group

    xa, xb, tables = spread(search, images)
    vmem, anywhere = pl.BlockSpec(memory_space=pltpu.VMEM), pl.BlockSpec(memory_space=pl.ANY)
    bf16, f32, dma = jnp.bfloat16, jnp.float32, pltpu.SemaphoreType.DMA
    peers = SIDE - 1
    weighted, loglik = pl.pallas_call(
        main_kernel,
        out_shape=(
            jax.ShapeDtypeStruct((oris, slice_columns), bf16),
            jax.ShapeDtypeStruct((groups, images_plane), f32),
        ),
        in_specs=[vmem, anywhere, anywhere, anywhere],
        out_specs=(vmem, vmem),
        scratch_shapes=[
            pltpu.VMEM((SIDE, planes, rows, half), bf16),
            pltpu.VMEM((SIDE, planes, rows, half), bf16),
            pltpu.VMEM((oris, slice_columns), bf16),
            pltpu.VMEM((2, SIDE, SLOTS, SIDE, planes, LANES), f32),
            pltpu.VMEM((SIDE, CORES, SLOTS, SIDE, SIDE, group, slice_columns), bf16),
            pltpu.VMEM((2, peers, CORES, SLOTS, SIDE, group, half), bf16),
            pltpu.VMEM((2, peers, CORES, SLOTS, SIDE, group, half), bf16),
            pltpu.VMEM((2, oris, lanes), f32),
            pltpu.VMEM((SIDE, oris, lanes), f32),
            pltpu.VMEM((SIDE, oris, lanes), f32),
            pltpu.VMEM((peers, oris, lanes), f32),
            pltpu.VMEM((blocks, 8, lanes), f32),
            pltpu.VMEM((SIDE, CORES, oris, lanes), bf16),
            pltpu.VMEM((oris, slice_columns), f32),
            dma((3,)),
            dma((2, peers)),
            dma((SIDE, peers)),
            dma((2, peers)),
            dma((SIDE, peers)),
            dma((2,)),
            dma((SIDE,)),
            dma((peers,)),
            dma((peers,)),
            dma((blocks,)),
            dma((blocks,)),
            dma((SIDE,)),
            dma((SIDE,)),
            dma((SIDE,)),
            dma((SIDE,)),
        ],
        compiler_params=pltpu.CompilerParams(collective_id=1, has_side_effects=True, vmem_limit_bytes=62 * 2**20),
        cost_estimate=pl.CostEstimate(flops=15 * 10**9, bytes_accessed=32 * 2**20, transcendentals=10**6),
    )(tables, xa, xb, projections)
    b = lax.axis_index("ori")
    home = lax.rem(b, SIDE) * SIDE + lax.div(b, SIDE)
    loglik = lax.dynamic_index_in_dim(loglik.reshape(groups, blocks, group), home, 1, False)
    return weighted, loglik.reshape(-1)


def solution(mesh):
    placed = (P(("img", "ori"), None), P("ori", None), P(("img", "ori"), None))
    return jax.shard_map(
        per_device,
        mesh=mesh,
        in_specs=placed,
        out_specs=(P("ori", "img"), P(("img", "ori"))),
        check_vma=False,
    )
```

time: 494 us -> 189 us (0.38)
  waiting for transfers between devices: 377 us -> 0 us
  Pallas kernels: 0 us -> 184 us
  starting transfers between devices: 32.6 us -> 0 us
  matrix products: 31.2 us -> 0 us
  other arithmetic: 25.4 us -> 0 us
  between operations: 14.2 us -> 0.65 us
  local copies, waits for them, and re-layouts: 13 us -> 4.16 us
    all_to_all x5 -> x0, waiting for transfers between devices: 227 us -> none  [the longest x1 208 us: per_device(): lax.all_to_all(outgoing, 'ori', split_axis=0, concat_axis=0, tiled=True)]
    pallas_call x0 -> x2, Pallas kernels: none -> 184 us  [the longest x1 137 us: per_device(): pl.pallas_call(main_kernel, out_shape=(jax.ShapeDtypeStruct((oris, slice_...]
    reduce_scatter x1 -> x0, waiting for transfers between devices: 149 us -> none  [per_device(): lax.psum_scatter(partial_sum, 'img', scatter_dimension=1, tiled=True)]
    all_to_all x5 -> x0, starting transfers between devices: 32.4 us -> none  [the longest x1 13.4 us: per_device(): lax.all_to_all(local_sum, 'ori', split_axis=0, concat_axis=0, tiled=True)]
    dot_general x2 -> x0, matrix products: 31.2 us -> none  [the longest x1 16.1 us: per_device(): lax.dot_general(responsibility, flat_images, (((0,), (0,)), ((), ())), pr...]
    mul x4 -> x0, other arithmetic: 11.2 us -> none  [the longest x1 10.6 us: per_device(): outgoing = grouped[source] * in_use.astype(jnp.bfloat16)[:, None, None]]
    reduce_sum x5 -> x0, other arithmetic: 8.62 us -> none  [the longest x1 7.88 us: per_device(): jnp.sum(jnp.square(projections.astype(jnp.float32)), axis=1)]
    gather x5 -> x0, local copies, waits for them, and re-layouts: 8.3 us -> none  [the longest x1 6.53 us: per_device(): outgoing = grouped[source] * in_use.astype(jnp.bfloat16)[:, None, None]]
  transfers between devices with their start and end apart: 6 -> 0, of which waited for: 6 -> 0; matrix products, arithmetic and copies ran while one was open for 3% -> 0% of each run, Pallas kernels for 0% -> 0%
where the time goes in v1:
time: 189 us
  Pallas kernels  184 us (97%)
  local copies, waits for them, and re-layouts  4.16 us (2%)
    pallas_call x1, Pallas kernels, per_device(): pl.pallas_call(main_kernel, out_shape=(jax.ShapeDtypeStruct((oris, slice_...  137 us
    pallas_call x1, Pallas kernels, spread(): pl.pallas_call(spread_kernel, out_shape=(line, line, jax.ShapeDtypeStruct...  46.9 us

profile of v1, /device:TPU:1, one launch (start us, length us, event | category | flops | bytes accessed | tf_op | source)
XLA Modules:
  0.0 188.9 jit_solution(8992840534716759407)
XLA Ops:
  0.6 46.9 %shard_map.50 = (bf16[4,8,64,768]{3,2,1,0:T(8,128)(2,1)}, bf16[4,8,64,768]{3,2,1,0:T(8,128)(2,1)}, f32[16,8,128]{2,1,0:T(8,128)}) custom-call(s32[4,4]{1,0:T(4,128)} %search.1, bf16[64,12288]{1,0:T(8,128)(2,1)} %images.1), custom_call_target="tpu_custom_call" | custom-call | bytes 16777216 | tf_op jit(solution)/shard_map/pallas_call | solution.py:189
  47.5 137.2 %shard_map.51 = (bf16[576,1536]{1,0:T(8,128)(2,1)}, f32[4,256]{1,0:T(4,128)}) custom-call(f32[16,8,128]{2,1,0:T(8,128)} %get-tuple-element.7.tables, bf16[4,8,64,768]{3,2,1,0:T(8,128)(2,1)} %get-tuple-element.8.xa_hbm, bf16[4,8,64,768]{3,2,1,0:T(8,128)(2,1)} %get-tuple-element.9.xb_hbm, bf16[576,12288]{1,0:T(8,128)(2,1)} %projections.1), custom_call_target="tpu_custom_call" | custom-call | flops 15000000512 | bytes 33554432 | tf_op jit(solution)/shard_map/pallas_call | solution.py:487
  184.7 0.8 reshape.11
  185.5 0.6 reshape.12
  186.1 2.8 %copy.8 = bf16[576,1536]{1,0:T(8,128)(2,1)} copy(bf16[576,1536]{1,0:T(8,128)(2,1)} %get-tuple-element.14) | data formatting | bytes 3538944
  (1 shorter events, 0.0 us)

commit v2 on v0

v2 whole, which is shorter than its diff:
```python
import jax
import jax.numpy as jnp
from jax import lax
from jax.experimental import pallas as pl
from jax.experimental.pallas import tpu as pltpu
from jax.sharding import PartitionSpec as P

MESH = pl.DeviceIdType.MESH
SIDE = 4
CORES = 2
PLANES = SIDE * CORES
BLOCKS = SIDE * SIDE
SLOTS = 2
LANES = 128
BATCHES = 2
AHEAD = 3
NO_SCORE = -3.0e38

ROUNDS = [(2, 2), (1, 3), (3, 1), (0, 0)]


def ring(position, step):
    return lax.rem(position + step + SIDE, SIDE)


def at_img(y, c):
    return {"img": y * CORES + c, "ori": lax.axis_index("ori")}


def at_ori(x, z):
    return {"img": lax.axis_index("img"), "ori": x * SIDE + z}


def remote(source, target, send, recv, device):
    return pltpu.make_async_remote_copy(
        src_ref=source,
        dst_ref=target,
        send_sem=send,
        recv_sem=recv,
        device_id=device,
        device_id_type=MESH,
    )


def greet(devices):
    barrier = pltpu.get_barrier_semaphore()
    for device in devices:
        pl.semaphore_signal(barrier, inc=1, device_id=device, device_id_type=MESH)
    pl.semaphore_wait(barrier, len(devices))


def slot_table(search):
    lane = lax.broadcasted_iota(jnp.int32, (8, LANES), 1)
    b, s = lax.rem(lane, BLOCKS), lax.div(lane, BLOCKS)
    table = jnp.full((8, LANES), -1.0, jnp.float32)
    rank = jnp.zeros((8, LANES), jnp.int32)
    for g in range(search.shape[0]):
        hit = b == search[g, 0]
        for n in range(1, search.shape[1]):
            hit = hit | (b == search[g, n])
        table = jnp.where(hit & (rank == s), float(g), table)
        rank = rank + hit.astype(jnp.int32)
    return table


def kernel(
    search,
    images,
    projections,
    weighted,
    loglik,
    xa,
    xb,
    told,
    tables,
    picks,
    proj,
    arrived,
    out_a,
    out_b,
    pair_out,
    pair_in,
    kept,
    y_in,
    stats,
    resp,
    total,
    load_sem,
    turn_send,
    turn_recv,
    told_send,
    told_recv,
    table_send,
    table_recv,
    near_send,
    near_recv,
    far_send,
    far_recv,
    a_send,
    a_recv,
    b_send,
    b_recv,
    pair_send,
    pair_recv,
    y_send,
    y_recv,
    stat_send,
    stat_recv,
    r_send,
    r_recv,
    rc_send,
    rc_recv,
):
    me, block = lax.axis_index("img"), lax.axis_index("ori")
    y, c = lax.div(me, CORES), lax.rem(me, CORES)
    x, z = lax.div(block, SIDE), lax.rem(block, SIDE)
    other = 1 - c
    rows, half = xa.shape[2], xa.shape[3]
    mid = rows // 2
    group = arrived.shape[7]
    groups = rows // group
    slice_columns = 2 * half
    lanes = kept.shape[3]
    partner = at_img(y, other)
    steps = [(dx, dz) for dx in range(SIDE) for dz in range(SIDE) if (dx, dz) != (0, 0)]
    ori_peers = [at_ori(ring(x, dx), ring(z, dz)) for dx, dz in steps]
    img_peers = [partner] + [at_img(ring(y, d), cc) for d in range(1, SIDE) for cc in range(CORES)]
    neighbours = [at_ori(ring(x, 1), z), at_ori(ring(x, -1), z), at_ori(x, ring(z, 1)), at_ori(x, ring(z, -1))]


    def columns(m, part):
        return images.at[:, pl.ds(pl.multiple_of(m * slice_columns + part * half, LANES), half)]

    def line(part):
        return (xa, x) if part == 0 else (xb, z)

    home = []
    for part in range(2):
        ref, place = line(part)
        home.append(pltpu.make_async_copy(columns(me, part), ref.at[place, me], load_sem.at[part]))
    load = pltpu.make_async_copy(
        projections.at[:, pl.ds(pl.multiple_of(me * slice_columns, LANES), slice_columns)], proj, load_sem.at[2]
    )
    for copy in home + [load]:
        copy.start()
    told[me] = slot_table(search)
    greet(img_peers + ori_peers)
    receivers = [(0, other)] + [(d, cc) for d in (2, 1 + 2 * c, 3 - 2 * c) for cc in range(CORES)]
    tells, turns = [], {}
    for k, (d, cc) in enumerate(receivers):
        tells.append(remote(told.at[me], told.at[me], told_send.at[k], told_recv.at[d, c], at_img(ring(y, -d), cc)))
        tells[-1].start()
    for k, (d, cc) in enumerate(receivers):
        for part in range(2):
            ref, place = line(part)
            turns[k, part] = remote(
                columns(ring(y, -d) * CORES + cc, part),
                ref.at[place, me],
                turn_send.at[k, part],
                turn_recv.at[d, c, part],
                at_img(ring(y, -d), cc),
            )
            turns[k, part].start()

    sources = [(0, c), (0, other), (2, 0), (2, 1), (1, 0), (3, 1), (3, 0), (1, 1)]

    def source(k):
        d, cc = sources[k]
        return ring(y, d) * CORES + cc

    near, far = {}, {}

    def start_near(k):
        d, cc = sources[k]
        for part in range(2):
            ref, place = line(part)
            block_ref = ref.at[place, source(k)]
            if k == 0:
                home[part].wait()
            else:
                remote(
                    block_ref, block_ref, turn_send.at[k - 1, part], turn_recv.at[d, cc, part], partner
                ).wait_recv()
            for way in (2 * part, 2 * part + 1):
                near[k, way] = remote(
                    block_ref, block_ref, near_send.at[k, way], near_recv.at[k, way], neighbours[way]
                )
                near[k, way].start()

    def start_far(k):
        for way in range(4):
            ref, place = line(way // 2)
            forward = way % 2 == 0
            near[k, way].wait_recv()
            block_ref = ref.at[ring(place, -1 if forward else 1), source(k), pl.ds(0 if forward else mid, mid)]
            far[k, way] = remote(block_ref, block_ref, far_send.at[k, way], far_recv.at[k, way], neighbours[way])
            far[k, way].start()

    def wait_far(k):
        for way in range(4):
            far[k, way].wait_recv()

    start_near(0)
    for d in range(SIDE):
        for cc in range(CORES) if d else (other,):
            tile = told.at[ring(y, d) * CORES + cc]
            remote(tile, tile, told_send.at[0], told_recv.at[d, cc], partner).wait_recv()
    sublane = lax.broadcasted_iota(jnp.int32, (PLANES, LANES), 0)
    gathered = told[0]
    for m in range(1, PLANES):
        gathered = jnp.where(sublane == m, told[m], gathered)
    tables[block] = gathered
    spreads = [
        remote(tables.at[block], tables.at[block], table_send.at[k], table_recv.at[k], peer)
        for k, peer in enumerate(ori_peers)
    ]
    for copy in spreads:
        copy.start()
    start_near(1)
    start_far(0)
    start_near(2)
    start_far(1)
    start_near(3)
    start_far(2)
    for copy in spreads:
        copy.wait_recv()
    lane_row = lax.broadcasted_iota(jnp.int32, (LANES, LANES), 0)
    homes = [
        jnp.concatenate([tables[p * SIDE + z] for p in range(SIDE)], axis=0),
        jnp.concatenate([tables[x * SIDE + p] for p in range(SIDE)], axis=0),
    ]
    for d in range(SIDE):
        for s in range(SLOTS):
            for part, dest in enumerate((x * SIDE + ring(z, d), ring(x, d) * SIDE + z)):
                column = jnp.where(lane_row == s * BLOCKS + dest, 1.0, 0.0)
                pick = jnp.dot(homes[part], column, preferred_element_type=jnp.float32)
                for p in range(SIDE):
                    picks[part, d, s, p] = pick[p * PLANES : (p + 1) * PLANES]
    start_near(4)
    start_far(3)


    order = [(q, r) for q in range(BATCHES) for r in range(SIDE)]

    def fill(n):
        q, r = order[n]
        slot = n % AHEAD
        near_y, far_y = ring(y, ROUNDS[r][0]), ring(y, ROUNDS[r][1])

        def step(i, carry):
            cc, t = lax.div(i, 2), lax.rem(i, 2)
            m = (near_y + (far_y - near_y) * cc) * CORES + cc
            for part, (ref, place) in enumerate(((xa, z), (xb, x))):
                odd = lax.rem(place + q, 2)
                p = 2 * t + odd
                choices = [ref[p, m, g * group : (g + 1) * group, :] for g in range(groups)]
                for d in range(SIDE):
                    for s in range(SLOTS):
                        pick = jnp.broadcast_to(picks[part, d, s, p, pl.ds(m, 1), :], (group, LANES))
                        pick = jnp.concatenate([pick.astype(jnp.bfloat16)] * (half // LANES), axis=1)
                        value = choices[0]
                        for g in range(1, groups):
                            value = jnp.where(pick == g, choices[g], value)
                        if d and part == 0:
                            out_a[slot, d - 1, cc, s, t] = value
                        elif d:
                            out_b[slot, d - 1, cc, s, t] = value
                        elif part == 0:
                            arrived[q, r, cc, s, lax.div(z, 2), lax.rem(z, 2), t, :, 0:half] = value
                        else:
                            arrived[q, r, cc, s, t, odd, lax.div(x, 2), :, half : 2 * half] = value
            return carry

        lax.fori_loop(0, CORES * 2, step, 0)

    moves = {}

    def send(n):
        q, r = order[n]
        slot = n % AHEAD
        moves[n] = []
        for d in (2, 1, 3):
            moves[n].append(
                remote(
                    out_a.at[slot, d - 1],
                    arrived.at[q, r, :, :, lax.div(z, 2), lax.rem(z, 2), :, :, pl.ds(0, half)],
                    a_send.at[slot, d - 1],
                    a_recv.at[n, d - 1],
                    at_ori(x, ring(z, d)),
                )
            )
            moves[n].append(
                remote(
                    out_b.at[slot, d - 1],
                    arrived.at[q, r, :, :, :, lax.rem(x + q, 2), lax.div(x, 2), :, pl.ds(half, half)],
                    b_send.at[slot, d - 1],
                    b_recv.at[n, d - 1],
                    at_ori(ring(x, d), z),
                )
            )
        for copy in moves[n]:
            copy.start()

    start_near(5)
    start_far(4)
    wait_far(2)
    wait_far(3)
    fill(0)
    send(0)
    start_near(6)
    start_far(5)
    start_near(7)
    wait_far(4)
    wait_far(5)
    fill(1)
    send(1)
    start_far(6)
    start_far(7)
    for copy in tells + list(turns.values()) + spreads:
        copy.wait_send()
    load.wait()
    wide = proj[...].astype(jnp.float32)
    half_norm = 0.5 * jnp.sum(wide * wide, axis=1, keepdims=True)
    wait_far(6)
    wait_far(7)
    if AHEAD > 2:
        fill(2)
        send(2)
    wait_far(0)
    wait_far(1)

    def scores(q, r, cc):
        values = arrived[q, r, cc].reshape(lanes, slice_columns)
        return (
            lax.dot_general(proj[...], values, (((1,), (1,)), ((), ())), preferred_element_type=jnp.float32)
            - half_norm
        )

    pairs, sums = {}, {}

    def round_of(n):
        q, r = order[n]
        for copy in moves[n]:
            copy.wait_recv()
        if n + AHEAD < len(order):
            for copy in moves[n]:
                copy.wait_send()
            fill(n + AHEAD)
            send(n + AHEAD)
        slot = n % 2
        if n >= 2:
            pairs[n - 2].wait_send()
        pair_out[slot] = scores(q, r, other)
        pairs[n] = remote(pair_out.at[slot], pair_in.at[n], pair_send.at[slot], pair_recv.at[n], partner)
        pairs[n].start()
        kept[q, r] = scores(q, r, c)
        pairs[n].wait_recv()
        kept[q, r] += pair_in[n]
        if r < SIDE - 1:
            d = ROUNDS[r][0] + (ROUNDS[r][1] - ROUNDS[r][0]) * c
            sums[n] = remote(kept.at[q, r], y_in.at[q, d - 1], y_send.at[q, r], y_recv.at[q, d - 1], at_img(ring(y, d), c))
            sums[n].start()


    last = SIDE - 1
    shares = {}

    def share(q):
        for n in range(q * SIDE, q * SIDE + last):
            sums[n].wait_recv()
        kept[q, last] = kept[q, last] + y_in[q, 0] + y_in[q, 1] + y_in[q, 2]
        highest = jnp.max(kept[q, last], axis=0, keepdims=True)
        mass = jnp.sum(jnp.exp(kept[q, last] - highest), axis=0, keepdims=True)
        which = lax.broadcasted_iota(jnp.int32, (8, lanes), 0)
        stats[q, block] = jnp.where(which == 0, highest, mass)
        shares[q] = [
            remote(stats.at[q, block], stats.at[q, block], stat_send.at[q, k], stat_recv.at[q, k], peer)
            for k, peer in enumerate(ori_peers)
        ]
        for copy in shares[q]:
            copy.start()

    images_batch = lanes // SLOTS
    home_row = lax.broadcasted_iota(jnp.int32, (BLOCKS, images_batch), 0)
    home_lane = lax.broadcasted_iota(jnp.int32, (BLOCKS, images_batch), 1)
    lane_z, lane_t = lax.div(home_lane, 2 * group), lax.rem(lax.div(home_lane, group), 2)
    block_row = lax.broadcasted_iota(jnp.int32, (BLOCKS, lanes), 0)

    def respond(q):
        spot = (2 * lane_t + lax.rem(lane_z + q, 2)) * SIDE + lane_z
        widen = jnp.where(home_row == spot, 1.0, 0.0)
        plane = tables[:, pl.ds(me, 1), :].reshape(BLOCKS, LANES)
        named = lax.dot_general(plane, widen, (((0,), (0,)), ((), ())), preferred_element_type=jnp.float32)
        named = jnp.concatenate([named[s * BLOCKS : (s + 1) * BLOCKS] for s in range(SLOTS)], axis=1)
        own = jnp.sum(jnp.where(block_row == block, named, 0.0), axis=0, keepdims=True)
        for copy in shares[q]:
            copy.wait()
        tops, masses = stats[q, :, 0, :], stats[q, :, 1, :]
        norm = jnp.zeros((1, lanes), jnp.float32)
        for g in range(groups):
            listed = named == g
            top = jnp.max(jnp.where(listed, tops, NO_SCORE), axis=0, keepdims=True)
            top = jnp.maximum(top[:, :images_batch], top[:, images_batch:])
            top2 = jnp.concatenate([top, top], axis=1)
            mass = jnp.where(listed, jnp.exp(jnp.minimum(tops - top2, 0.0)) * masses, 0.0)
            mass = jnp.sum(mass, axis=0, keepdims=True)
            value = top + jnp.log(mass[:, :images_batch] + mass[:, images_batch:])
            loglik[q, pl.ds(g, 1), :] = value
            norm = jnp.where(own == g, jnp.concatenate([value, value], axis=1), norm)
        value = jnp.where(own >= 0, jnp.exp(kept[q, last] - norm), 0.0).astype(jnp.bfloat16)
        for h in range(2):
            resp[q, 0, c, h] = value[:, h * LANES : (h + 1) * LANES]


    direct, passed, crossed = {}, {}, {}

    def cross(q, d):
        crossed[q, d] = remote(resp.at[q, d, c], resp.at[q, d, c], rc_send.at[q, d], rc_recv.at[q, d], partner)
        crossed[q, d].start()

    def gather_near(q):
        for step in range(2):
            for d, h in ((1, step), (3, 1 - step)):
                direct[q, d, h] = remote(
                    resp.at[q, 0, c, h], resp.at[q, d, c, h], r_send.at[q, d, h], r_recv.at[q, d, h], at_img(ring(y, -d), c)
                )
                direct[q, d, h].start()
        cross(q, 0)

    def gather_far(q):
        for d, h in ((1, 0), (3, 1)):
            direct[q, d, h].wait_recv()
            passed[q, h] = remote(
                resp.at[q, d, c, h], resp.at[q, 2, c, h], r_send.at[q, 2, h], r_recv.at[q, 2, h], at_img(ring(y, -d), c)
            )
            passed[q, h].start()
        for d, h in ((1, 1), (3, 0)):
            direct[q, d, h].wait_recv()
            cross(q, d)

    def gather_last(q):
        for h in range(2):
            passed[q, h].wait_recv()
        cross(q, 2)

    tile = 2 * LANES

    def add(q, d, first=False, final=False):
        crossed[q, d].wait_recv()
        for t in range(slice_columns // tile):
            cols = slice(t * tile, (t + 1) * tile)
            part = None if first else total[:, cols]
            for cc in range(CORES):
                r = [pair[cc] for pair in ROUNDS].index(d)
                factor = jnp.concatenate([resp[q, d, cc, 0], resp[q, d, cc, 1]], axis=1)
                values = arrived[q, r, cc, :, :, :, :, :, cols].reshape(lanes, tile)
                product = jnp.dot(factor, values, preferred_element_type=jnp.float32)
                part = product if part is None else part + product
            if final:
                weighted[:, cols] = part.astype(weighted.dtype)
            else:
                total[:, cols] = part

    for n in range(4):
        round_of(n)
    share(0)
    round_of(4)
    respond(0)
    gather_near(0)
    round_of(5)
    gather_far(0)
    add(0, 0, first=True)
    round_of(6)
    gather_last(0)
    add(0, 1)
    round_of(7)
    share(1)
    add(0, 3)
    add(0, 2)
    respond(1)
    gather_near(1)
    add(1, 0)
    gather_far(1)
    add(1, 1)
    add(1, 3)
    gather_last(1)
    add(1, 2, final=True)

    for copy in list(near.values()) + list(far.values()):
        copy.wait_send()
    for n in range(len(order) - AHEAD, len(order)):
        for copy in moves[n]:
            copy.wait_send()
    for n in (len(order) - 2, len(order) - 1):
        pairs[n].wait_send()
    for copies in (sums, direct, passed, crossed):
        for copy in copies.values():
            copy.wait_send()


def per_device(images, projections, search):
    groups, _ = search.shape
    rows, columns = images.shape
    group = rows // groups
    slice_columns = columns // PLANES
    half = slice_columns // 2
    oris = projections.shape[0]
    lanes = BLOCKS * SLOTS * group // BATCHES
    peers, rounds = SIDE - 1, BATCHES * SIDE

    vmem, anywhere = pl.BlockSpec(memory_space=pltpu.VMEM), pl.BlockSpec(memory_space=pl.ANY)
    bf16, f32, dma = jnp.bfloat16, jnp.float32, pltpu.SemaphoreType.DMA
    weighted, loglik = pl.pallas_call(
        kernel,
        out_shape=(
            jax.ShapeDtypeStruct((oris, slice_columns), bf16),
            jax.ShapeDtypeStruct((BATCHES, groups, lanes // SLOTS), f32),
        ),
        in_specs=[pl.BlockSpec(memory_space=pltpu.SMEM), anywhere, anywhere],
        out_specs=(vmem, vmem),
        scratch_shapes=[
            pltpu.VMEM((SIDE, PLANES, rows, half), bf16),
            pltpu.VMEM((SIDE, PLANES, rows, half), bf16),
            pltpu.VMEM((PLANES, 8, LANES), f32),
            pltpu.VMEM((BLOCKS, PLANES, LANES), f32),
            pltpu.VMEM((2, SIDE, SLOTS, SIDE, PLANES, LANES), f32),
            pltpu.VMEM((oris, slice_columns), bf16),
            pltpu.VMEM((BATCHES, SIDE, CORES, SLOTS, 2, 2, 2, group, slice_columns), bf16),
            pltpu.VMEM((AHEAD, peers, CORES, SLOTS, 2, group, half), bf16),
            pltpu.VMEM((AHEAD, peers, CORES, SLOTS, 2, group, half), bf16),
            pltpu.VMEM((2, oris, lanes), f32),
            pltpu.VMEM((rounds, oris, lanes), f32),
            pltpu.VMEM((BATCHES, SIDE, oris, lanes), f32),
            pltpu.VMEM((BATCHES, peers, oris, lanes), f32),
            pltpu.VMEM((BATCHES, BLOCKS, 8, lanes), f32),
            pltpu.VMEM((BATCHES, SIDE, CORES, 2, oris, LANES), bf16),
            pltpu.VMEM((oris, slice_columns), f32),
            dma((3,)),
            dma((PLANES - 1, 2)),
            dma((SIDE, CORES, 2)),
            dma((PLANES - 1,)),
            dma((SIDE, CORES)),
            dma((BLOCKS - 1,)),
            dma((BLOCKS - 1,)),
            dma((PLANES, 4)),
            dma((PLANES, 4)),
            dma((PLANES, 4)),
            dma((PLANES, 4)),
            dma((AHEAD, peers)),
            dma((rounds, peers)),
            dma((AHEAD, peers)),
            dma((rounds, peers)),
            dma((2,)),
            dma((rounds,)),
            dma((BATCHES, peers)),
            dma((BATCHES, peers)),
            dma((BATCHES, BLOCKS - 1)),
            dma((BATCHES, BLOCKS - 1)),
            dma((BATCHES, SIDE, 2)),
            dma((BATCHES, SIDE, 2)),
            dma((BATCHES, SIDE)),
            dma((BATCHES, SIDE)),
        ],
        compiler_params=pltpu.CompilerParams(collective_id=0, has_side_effects=True, vmem_limit_bytes=62 * 2**20),
        cost_estimate=pl.CostEstimate(flops=15 * 10**9, bytes_accessed=32 * 2**20, transcendentals=10**6),
    )(search, images, projections)
    b = lax.axis_index("ori")
    x, z = lax.div(b, SIDE), lax.rem(b, SIDE)
    start = z * (2 * group) + lax.div(x, 2) * group
    loglik = lax.dynamic_slice(loglik, (lax.rem(x + z, BATCHES), 0, start), (1, groups, group))
    return weighted, loglik.reshape(-1)


def solution(mesh):
    placed = (P(("img", "ori"), None), P("ori", None), P(("img", "ori"), None))
    return jax.shard_map(
        per_device,
        mesh=mesh,
        in_specs=placed,
        out_specs=(P("ori", "img"), P(("img", "ori"))),
        check_vma=False,
    )
```

time: 494 us -> 167 us (0.34)
  waiting for transfers between devices: 377 us -> 0 us
  Pallas kernels: 0 us -> 162 us
  starting transfers between devices: 32.6 us -> 0 us
  matrix products: 31.2 us -> 0 us
  other arithmetic: 25.4 us -> 0 us
  between operations: 14.2 us -> 0.67 us
  local copies, waits for them, and re-layouts: 13 us -> 4.11 us
    all_to_all x5 -> x0, waiting for transfers between devices: 227 us -> none  [the longest x1 208 us: per_device(): lax.all_to_all(outgoing, 'ori', split_axis=0, concat_axis=0, tiled=True)]
    pallas_call x0 -> x1, Pallas kernels: none -> 162 us  [per_device(): pl.pallas_call(kernel, out_shape=(jax.ShapeDtypeStruct((oris, slice_colum...]
    reduce_scatter x1 -> x0, waiting for transfers between devices: 149 us -> none  [per_device(): lax.psum_scatter(partial_sum, 'img', scatter_dimension=1, tiled=True)]
    all_to_all x5 -> x0, starting transfers between devices: 32.4 us -> none  [the longest x1 13.4 us: per_device(): lax.all_to_all(local_sum, 'ori', split_axis=0, concat_axis=0, tiled=True)]
    dot_general x2 -> x0, matrix products: 31.2 us -> none  [the longest x1 16.1 us: per_device(): lax.dot_general(responsibility, flat_images, (((0,), (0,)), ((), ())), pr...]
    mul x4 -> x0, other arithmetic: 11.2 us -> none  [the longest x1 10.6 us: per_device(): outgoing = grouped[source] * in_use.astype(jnp.bfloat16)[:, None, None]]
    reduce_sum x5 -> x0, other arithmetic: 8.62 us -> none  [the longest x1 7.88 us: per_device(): jnp.sum(jnp.square(projections.astype(jnp.float32)), axis=1)]
    gather x5 -> x0, local copies, waits for them, and re-layouts: 8.3 us -> none  [the longest x1 6.53 us: per_device(): outgoing = grouped[source] * in_use.astype(jnp.bfloat16)[:, None, None]]
  transfers between devices with their start and end apart: 6 -> 0, of which waited for: 6 -> 0; matrix products, arithmetic and copies ran while one was open for 3% -> 0% of each run, Pallas kernels for 0% -> 0%
where the time goes in v2:
time: 167 us
  Pallas kernels  162 us (97%)
  local copies, waits for them, and re-layouts  4.11 us (2%)
    pallas_call x1, Pallas kernels, per_device(): pl.pallas_call(kernel, out_shape=(jax.ShapeDtypeStruct((oris, slice_colum...  162 us

profile of v2, /device:TPU:1, one launch (start us, length us, event | category | flops | bytes accessed | tf_op | source)
XLA Modules:
  0.0 167.0 jit_solution(3220156010376318577)
XLA Ops:
  0.7 162.3 %shard_map.50 = (bf16[576,1536]{1,0:T(8,128)(2,1)}, f32[2,4,128]{2,1,0:T(4,128)}) custom-call(s32[4,4]{1,0:T(4,128)} %search.1, bf16[64,12288]{1,0:T(8,128)(2,1)} %images.1, bf16[576,12288]{1,0:T(8,128)(2,1)} %projections.1), custom_call_target="tpu_custom_call" | custom-call | flops 15000000512 | bytes 33554432 | tf_op jit(solution)/shard_map/pallas_call | solution.py:513
  162.9 0.7 constant_dynamic-slice_fusion
  163.7 0.6 reshape.7
  164.3 2.8 %copy.6 = bf16[576,1536]{1,0:T(8,128)(2,1)} copy(bf16[576,1536]{1,0:T(8,128)(2,1)} %get-tuple-element.8) | data formatting | bytes 3538944

commit v3 on v2

v3 whole, which is shorter than its diff:
```python
import jax
import jax.numpy as jnp
from jax import lax
from jax.experimental import pallas as pl
from jax.experimental.pallas import tpu as pltpu
from jax.sharding import PartitionSpec as P

MESH = pl.DeviceIdType.MESH
SIDE = 4
CORES = 2
PLANES = SIDE * CORES
BLOCKS = SIDE * SIDE
SLOTS = 2
LANES = 128
BATCHES = SIDE
AHEAD = 3
NO_SCORE = -3.0e38

ROUNDS = [(2, 2), (1, 3), (3, 1), (0, 0)]
ORDER = [(0, 3), (0, 1), (0, 2), (1, 3), (0, 0), (1, 0), (1, 1), (1, 2)] + [(q, r) for q in (2, 3) for r in range(4)]
RELAYED = (1, 2, 3)


def ring(position, step):
    return lax.rem(position + step + SIDE, SIDE)


def at_img(y, c):
    return {"img": y * CORES + c, "ori": lax.axis_index("ori")}


def at_ori(x, z):
    return {"img": lax.axis_index("img"), "ori": x * SIDE + z}


def remote(source, target, send, recv, device):
    return pltpu.make_async_remote_copy(
        src_ref=source,
        dst_ref=target,
        send_sem=send,
        recv_sem=recv,
        device_id=device,
        device_id_type=MESH,
    )


def greet(devices):
    barrier = pltpu.get_barrier_semaphore()
    for device in devices:
        pl.semaphore_signal(barrier, inc=1, device_id=device, device_id_type=MESH)
    pl.semaphore_wait(barrier, len(devices))


def slot_table(search):
    lane = lax.broadcasted_iota(jnp.int32, (8, LANES), 1)
    b, s = lax.rem(lane, BLOCKS), lax.div(lane, BLOCKS)
    table = jnp.full((8, LANES), -1.0, jnp.float32)
    rank = jnp.zeros((8, LANES), jnp.int32)
    for g in range(search.shape[0]):
        hit = b == search[g, 0]
        for n in range(1, search.shape[1]):
            hit = hit | (b == search[g, n])
        table = jnp.where(hit & (rank == s), float(g), table)
        rank = rank + hit.astype(jnp.int32)
    return table


def kernel(
    search,
    images,
    projections,
    weighted,
    loglik,
    xa,
    xb,
    told,
    tables,
    picks,
    proj,
    arrived,
    out_a,
    out_b,
    pair_out,
    pair_in,
    kept,
    y_half,
    y_in,
    stats,
    resp,
    scale,
    result,
    total,
    load_sem,
    turn_send,
    turn_recv,
    told_send,
    told_recv,
    table_send,
    table_recv,
    near_send,
    near_recv,
    far_send,
    far_recv,
    a_send,
    a_recv,
    b_send,
    b_recv,
    pair_send,
    pair_recv,
    h_send,
    h_recv,
    y_send,
    y_recv,
    stat_send,
    stat_recv,
    r_send,
    r_recv,
    rc_send,
    rc_recv,
    f_send,
    f_recv,
):
    me, block = lax.axis_index("img"), lax.axis_index("ori")
    y, c = lax.div(me, CORES), lax.rem(me, CORES)
    x, z = lax.div(block, SIDE), lax.rem(block, SIDE)
    other = 1 - c
    rows, half = xa.shape[2], xa.shape[3]
    mid = rows // 2
    group = arrived.shape[5]
    groups = rows // group
    slice_columns = 2 * half
    lanes = kept.shape[3]
    partner = at_img(y, other)
    steps = [(dx, dz) for dx in range(SIDE) for dz in range(SIDE) if (dx, dz) != (0, 0)]
    ori_peers = [at_ori(ring(x, dx), ring(z, dz)) for dx, dz in steps]
    img_peers = [partner] + [at_img(ring(y, d), cc) for d in range(1, SIDE) for cc in range(CORES)]
    neighbours = [at_ori(ring(x, 1), z), at_ori(ring(x, -1), z), at_ori(x, ring(z, 1)), at_ori(x, ring(z, -1))]


    def columns(m, part):
        return images.at[:, pl.ds(pl.multiple_of(m * slice_columns + part * half, LANES), half)]

    def line(part):
        return (xa, x) if part == 0 else (xb, z)

    home = []
    for part in range(2):
        ref, place = line(part)
        home.append(pltpu.make_async_copy(columns(me, part), ref.at[place, me], load_sem.at[part]))
    load = pltpu.make_async_copy(
        projections.at[:, pl.ds(pl.multiple_of(me * slice_columns, LANES), slice_columns)], proj, load_sem.at[2]
    )
    for copy in home + [load]:
        copy.start()
    told[me] = slot_table(search)
    greet(img_peers + ori_peers)
    receivers = [(0, other)] + [(d, cc) for d in (1 + 2 * c, 3 - 2 * c, 2) for cc in range(CORES)]
    tells, turns = [], {}
    for k, (d, cc) in enumerate(receivers):
        tells.append(remote(told.at[me], told.at[me], told_send.at[k], told_recv.at[d, c], at_img(ring(y, -d), cc)))
        tells[-1].start()

    def turn(ks):
        for k in ks:
            d, cc = receivers[k]
            for part in range(2):
                ref, place = line(part)
                turns[k, part] = remote(
                    columns(ring(y, -d) * CORES + cc, part),
                    ref.at[place, me],
                    turn_send.at[k, part],
                    turn_recv.at[d, c, part],
                    at_img(ring(y, -d), cc),
                )
                turns[k, part].start()

    turn(range(PLANES - 1))

    sources = [(0, c), (0, other), (1, 0), (3, 1), (3, 0), (1, 1), (2, 0), (2, 1)]

    def source(k):
        d, cc = sources[k]
        return ring(y, d) * CORES + cc

    near, far = {}, {}

    def start_near(k):
        d, cc = sources[k]
        for part in range(2):
            ref, place = line(part)
            block_ref = ref.at[place, source(k)]
            if k == 0:
                home[part].wait()
            else:
                remote(
                    block_ref, block_ref, turn_send.at[k - 1, part], turn_recv.at[d, cc, part], partner
                ).wait_recv()
            for way in (2 * part, 2 * part + 1):
                near[k, way] = remote(
                    block_ref, block_ref, near_send.at[k, way], near_recv.at[k, way], neighbours[way]
                )
                near[k, way].start()

    def start_far(k):
        for way in range(4):
            ref, place = line(way // 2)
            forward = way % 2 == 0
            near[k, way].wait_recv()
            block_ref = ref.at[ring(place, -1 if forward else 1), source(k), pl.ds(0 if forward else mid, mid)]
            far[k, way] = remote(block_ref, block_ref, far_send.at[k, way], far_recv.at[k, way], neighbours[way])
            far[k, way].start()

    def wait_far(k):
        for way in range(4):
            far[k, way].wait_recv()

    start_near(0)
    for d in range(SIDE):
        for cc in range(CORES) if d else (other,):
            tile = told.at[ring(y, d) * CORES + cc]
            remote(tile, tile, told_send.at[0], told_recv.at[d, cc], partner).wait_recv()
    sublane = lax.broadcasted_iota(jnp.int32, (PLANES, LANES), 0)
    gathered = told[0]
    for m in range(1, PLANES):
        gathered = jnp.where(sublane == m, told[m], gathered)
    tables[block] = gathered
    spreads = [
        remote(tables.at[block], tables.at[block], table_send.at[k], table_recv.at[k], peer)
        for k, peer in enumerate(ori_peers)
    ]
    for copy in spreads:
        copy.start()
    start_near(1)
    start_far(0)
    start_far(1)
    for copy in spreads:
        copy.wait_recv()
    lane_row = lax.broadcasted_iota(jnp.int32, (LANES, LANES), 0)
    homes = [
        jnp.concatenate([tables[p * SIDE + z] for p in range(SIDE)], axis=0),
        jnp.concatenate([tables[x * SIDE + p] for p in range(SIDE)], axis=0),
    ]
    for d in range(SIDE):
        for s in range(SLOTS):
            for part, dest in enumerate((x * SIDE + ring(z, d), ring(x, d) * SIDE + z)):
                column = jnp.where(lane_row == s * BLOCKS + dest, 1.0, 0.0)
                pick = jnp.dot(homes[part], column, preferred_element_type=jnp.float32)
                for p in range(SIDE):
                    picks[part, d, s, p] = pick[p * PLANES : (p + 1) * PLANES]


    order = ORDER

    def fill(n):
        q, r = order[n]
        slot = n % AHEAD
        ys = [ring(y, d) for d in ROUNDS[r]]

        def step(cc, carry):
            m = (ys[0] + (ys[1] - ys[0]) * cc) * CORES + cc
            for part, (ref, place) in enumerate(((xa, z), (xb, x))):
                p = ring(q, -place)
                choices = [ref[p, m, g * group : (g + 1) * group, :] for g in range(groups)]
                for d in range(SIDE):
                    for s in range(SLOTS):
                        pick = jnp.broadcast_to(picks[part, d, s, p, pl.ds(m, 1), :], (group, LANES))
                        pick = jnp.concatenate([pick.astype(jnp.bfloat16)] * (half // LANES), axis=1)
                        value = choices[0]
                        for g in range(1, groups):
                            value = jnp.where(pick == g, choices[g], value)
                        if d and part == 0:
                            out_a[slot, d - 1, cc, s] = value
                        elif d:
                            out_b[slot, d - 1, cc, s] = value
                        elif part == 0:
                            arrived[q, r, cc, s, z, :, 0:half] = value
                        else:
                            arrived[q, r, cc, s, p, :, half : 2 * half] = value
            return carry

        lax.fori_loop(0, CORES, step, 0)

    moves = {}

    def send(n):
        q, r = order[n]
        slot = n % AHEAD
        moves[n] = []
        for d in (2, 1, 3):
            moves[n].append(
                remote(
                    out_a.at[slot, d - 1],
                    arrived.at[q, r, :, :, z, :, pl.ds(0, half)],
                    a_send.at[slot, d - 1],
                    a_recv.at[n, d - 1],
                    at_ori(x, ring(z, d)),
                )
            )
            moves[n].append(
                remote(
                    out_b.at[slot, d - 1],
                    arrived.at[q, r, :, :, ring(q, -x), :, pl.ds(half, half)],
                    b_send.at[slot, d - 1],
                    b_recv.at[n, d - 1],
                    at_ori(ring(x, d), z),
                )
            )
        for copy in moves[n]:
            copy.start()

    wait_far(0)
    wait_far(1)
    fill(0)
    send(0)
    for k in range(2, 6):
        start_near(k)
    start_far(2)
    start_far(3)
    start_near(6)
    start_near(7)
    start_far(4)
    start_far(5)
    wait_far(2)
    wait_far(3)
    fill(1)
    send(1)
    start_far(6)
    start_far(7)
    wait_far(4)
    wait_far(5)
    fill(2)
    send(2)
    for copy in tells + list(turns.values()) + spreads:
        copy.wait_send()
    load.wait()
    wide = proj[...].astype(jnp.float32)
    half_norm = 0.5 * jnp.sum(wide * wide, axis=1, keepdims=True)


    pairs, sums, thirds = {}, {}, {}
    last = SIDE - 1
    mid_ori = kept.shape[2] // 2

    def refill(n):
        for copy in moves[n]:
            copy.wait_send()
        fill(n + AHEAD)
        send(n + AHEAD)

    def begin(n):
        q, r = order[n]
        slot = n % 2
        if n >= 2:
            pairs[n - 2].wait_send()
        values = arrived[q, r].reshape(CORES * lanes, slice_columns)
        value = lax.dot_general(proj[...], values, (((1,), (1,)), ((), ())), preferred_element_type=jnp.float32)
        value = value - half_norm
        for cc in range(CORES):
            pair_out[slot, cc] = value[:, cc * lanes : (cc + 1) * lanes]
        pairs[n] = remote(pair_out.at[slot, other], pair_in.at[n], pair_send.at[slot], pair_recv.at[n], partner)
        pairs[n].start()

    def finish(n):
        q, r = order[n]
        pairs[n].wait_recv()
        kept[q, r] = pair_out[n % 2, c] + pair_in[n]
        if r == 0 and q in RELAYED:
            for h, step in ((0, 1), (1, -1)):
                rows_h = pl.ds(h * mid_ori, mid_ori)
                thirds[q, h] = remote(
                    kept.at[q, r, rows_h], y_half.at[q, h], h_send.at[q, h], h_recv.at[q, h], at_img(ring(y, step), c)
                )
                thirds[q, h].start()
        elif r == 0:
            sums[n] = remote(kept.at[q, r], y_in.at[q, 2], y_send.at[q, 2], y_recv.at[q, 2], at_img(ring(y, 2), c))
            sums[n].start()
        elif r < last and q not in RELAYED:
            pass_on(n)

    def pass_on(n):
        q, r = order[n]
        d0, d1 = ROUNDS[r]
        d = d0 + (d1 - d0) * c
        h = lax.div(d, 2)
        if q in RELAYED:
            half_ref = y_half.at[q, h]
            remote(half_ref, half_ref, h_send.at[q, h], h_recv.at[q, h], partner).wait_recv()
            rows_h = pl.ds(pl.multiple_of(h * mid_ori, 8), mid_ori)
            kept[q, r, rows_h, :] = kept[q, r, rows_h, :] + y_half[q, h]
        sums[n] = remote(kept.at[q, r], y_in.at[q, h], y_send.at[q, h], y_recv.at[q, h], at_img(ring(y, d), c))
        sums[n].start()


    shares = {}

    def share(q):
        for n, copy in sums.items():
            if order[n][0] == q:
                copy.wait_recv()
        value = kept[q, last] + y_in[q, 0] + y_in[q, 1]
        if q not in RELAYED:
            value = value + y_in[q, 2]
        kept[q, last] = value
        highest = jnp.max(kept[q, last], axis=0, keepdims=True)
        value = jnp.exp(kept[q, last] - highest)
        resp[q, 0, c] = value.astype(jnp.bfloat16)
        mass = jnp.sum(value, axis=0, keepdims=True)
        which = lax.broadcasted_iota(jnp.int32, (8, lanes), 0)
        stats[q, block] = jnp.where(which == 0, highest, mass)
        shares[q] = [
            remote(stats.at[q, block], stats.at[q, block], stat_send.at[q, k], stat_recv.at[q, k], peer)
            for k, peer in enumerate(ori_peers)
        ]
        for copy in shares[q]:
            copy.start()

    images_batch = lanes // SLOTS
    home_row = lax.broadcasted_iota(jnp.int32, (BLOCKS, lanes), 0)
    home_lane = lax.broadcasted_iota(jnp.int32, (BLOCKS, lanes), 1)
    lane_z = lax.rem(lax.div(home_lane, group), SIDE)

    here = lax.rem(x + z, BATCHES)
    lane = lax.broadcasted_iota(jnp.int32, (1, lanes), 1)
    factors = {}

    def fold(value, operation):
        return operation(value, pltpu.roll(value, images_batch, 1))

    def respond(q):
        spot = lax.rem(q - lane_z + SIDE, SIDE) * SIDE + lane_z
        widen = jnp.where(home_row == spot, 1.0, 0.0)
        plane = tables[:, pl.ds(me, 1), :].reshape(BLOCKS, LANES)
        named = lax.dot_general(plane, widen, (((0,), (0,)), ((), ())), preferred_element_type=jnp.float32)
        named = jnp.where(home_lane < images_batch, named[:BLOCKS], named[BLOCKS : 2 * BLOCKS])
        own = jnp.sum(jnp.where(home_row == block, named, 0.0), axis=0, keepdims=True)
        for copy in shares[q]:
            copy.wait()
        tops, masses = stats[q, :, 0, :], stats[q, :, 1, :]
        norm = jnp.zeros((1, lanes), jnp.float32)
        row = jnp.zeros((1, lanes), jnp.float32) if q == 0 else result[...]
        for g in range(groups):
            listed = named == g
            top = fold(jnp.max(jnp.where(listed, tops, NO_SCORE), axis=0, keepdims=True), jnp.maximum)
            mass = jnp.where(listed, jnp.exp(jnp.minimum(tops - top, 0.0)) * masses, 0.0)
            mass = fold(jnp.sum(mass, axis=0, keepdims=True), jnp.add)
            value = top + jnp.log(mass)
            moved = pltpu.roll(value, lax.rem((g - z) * group + lanes, lanes), 1)
            row = jnp.where((lax.div(lane, group) == g) & (here == q), moved, row)
            norm = jnp.where(own == g, value, norm)
        result[...] = row
        value = jnp.where(own >= 0, jnp.exp(stats[q, pl.ds(block, 1), 0, :] - norm), 0.0)
        scale[q, 0, c] = jnp.broadcast_to(value, (8, lanes))
        factors[q] = []
        for k, (d, cc) in enumerate(receivers):
            factors[q].append(
                remote(
                    scale.at[q, 0, c], scale.at[q, d, c], f_send.at[q, k], f_recv.at[q, d, c], at_img(ring(y, -d), cc)
                )
            )
            factors[q][-1].start()


    direct, passed, crossed = {}, {}, {}

    def cross(q, d):
        crossed[q, d] = remote(resp.at[q, d, c], resp.at[q, d, c], rc_send.at[q, d], rc_recv.at[q, d], partner)
        crossed[q, d].start()

    def part_of(q, d, h):
        return resp.at[q, d, c, pl.ds(h * mid_ori, mid_ori)]

    def gather_near(q):
        cross(q, 0)
        for step in range(2):
            for d, h in ((1, step), (3, 1 - step)):
                direct[q, d, h] = remote(
                    part_of(q, 0, h), part_of(q, d, h), r_send.at[q, d, h], r_recv.at[q, d, h], at_img(ring(y, -d), c)
                )
                direct[q, d, h].start()

    def gather_direct(q):
        cross(q, 0)
        for d in (2, 1, 3):
            direct[q, d] = remote(
                resp.at[q, 0, c], resp.at[q, d, c], r_send.at[q, d, 0], r_recv.at[q, d, 0], at_img(ring(y, -d), c)
            )
            direct[q, d].start()

    def gather_far(q):
        for d, h in ((1, 0), (3, 1)):
            direct[q, d, h].wait_recv()
            passed[q, h] = remote(
                part_of(q, d, h), part_of(q, 2, h), r_send.at[q, 2, h], r_recv.at[q, 2, h], at_img(ring(y, -d), c)
            )
            passed[q, h].start()
        for d, h in ((1, 1), (3, 0)):
            direct[q, d, h].wait_recv()
            cross(q, d)

    def gather_last(q):
        for h in range(2):
            passed[q, h].wait_recv()
        cross(q, 2)

    tile = 2 * LANES

    def add(q, ds):
        for d in ds:
            crossed[q, d].wait_recv()
            for cc in range(CORES) if d else (other,):
                ref = scale.at[q, d, cc]
                remote(ref, ref, f_send.at[q, 0], f_recv.at[q, d, cc], partner).wait_recv()
        first, final = q == 0, q == BATCHES - 1 and 2 in ds
        pieces = [(d, cc) for d in ds for cc in range(CORES)]
        factor = jnp.concatenate(
            [(resp[q, d, cc].astype(jnp.float32) * scale[q, d, cc, 0:1, :]).astype(jnp.bfloat16) for d, cc in pieces], axis=1
        )
        for t in range(slice_columns // tile):
            cols = slice(t * tile, (t + 1) * tile)
            values = []
            for d, cc in pieces:
                r = [pair[cc] for pair in ROUNDS].index(d)
                values.append(arrived[q, r, cc, :, :, :, cols].reshape(lanes, tile))
            part = jnp.dot(factor, jnp.concatenate(values, axis=0), preferred_element_type=jnp.float32)
            if not first:
                part = part + total[:, cols]
            if final:
                weighted[:, cols] = part.astype(weighted.dtype)
            else:
                total[:, cols] = part

    shares_at, passes_at = {8: 0, 11: 1, 15: 2}, {8: (6, 7), 11: (9, 10), 13: (13,), 14: (14,)}
    for n in range(len(order)):
        for copy in moves[n]:
            copy.wait_recv()
        if n in shares_at:
            share(shares_at[n])
            gather_near(shares_at[n])
        if n == 1:
            wait_far(6)
            wait_far(7)
        if n + AHEAD < len(order):
            refill(n)
        begin(n)
        if 0 < n <= 12:
            finish(n - 1)
        if n >= 12:
            finish(n)
        for k in passes_at.get(n, ()):
            pass_on(k)
        if n == 9:
            gather_far(0)
        if n == 10:
            respond(0)
        if n == 11:
            gather_last(0)
        if n == 13:
            add(0, range(SIDE))
            gather_far(1)
        if n == 14:
            respond(1)
    gather_far(2)
    share(3)
    gather_direct(3)
    gather_last(1)
    add(1, range(SIDE))
    respond(2)
    gather_last(2)
    respond(3)
    add(2, range(SIDE))
    for d in (1, 3):
        direct[3, d].wait_recv()
        cross(3, d)
    add(3, (0, 1, 3))
    direct[3, 2].wait_recv()
    cross(3, 2)
    add(3, (2,))
    loglik[...] = result[:, 0 : loglik.shape[1]]

    for copy in list(near.values()) + list(far.values()):
        copy.wait_send()
    for n in range(len(order) - AHEAD, len(order)):
        for copy in moves[n]:
            copy.wait_send()
    for n in (len(order) - 2, len(order) - 1):
        pairs[n].wait_send()
    for q in range(BATCHES):
        for copy in factors[q]:
            copy.wait_send()
    for copies in (sums, thirds, direct, passed, crossed):
        for copy in copies.values():
            copy.wait_send()


def per_device(images, projections, search):
    groups, _ = search.shape
    rows, columns = images.shape
    group = rows // groups
    slice_columns = columns // PLANES
    half = slice_columns // 2
    oris = projections.shape[0]
    lanes = BLOCKS * SLOTS * group // BATCHES
    peers, rounds = SIDE - 1, BATCHES * SIDE
    mid_ori = oris // 2

    vmem, anywhere = pl.BlockSpec(memory_space=pltpu.VMEM), pl.BlockSpec(memory_space=pl.ANY)
    bf16, f32, dma = jnp.bfloat16, jnp.float32, pltpu.SemaphoreType.DMA
    weighted, loglik = pl.pallas_call(
        kernel,
        out_shape=(
            jax.ShapeDtypeStruct((oris, slice_columns), bf16),
            jax.ShapeDtypeStruct((1, rows), f32),
        ),
        in_specs=[pl.BlockSpec(memory_space=pltpu.SMEM), anywhere, anywhere],
        out_specs=(vmem, vmem),
        scratch_shapes=[
            pltpu.VMEM((SIDE, PLANES, rows, half), bf16),
            pltpu.VMEM((SIDE, PLANES, rows, half), bf16),
            pltpu.VMEM((PLANES, 8, LANES), f32),
            pltpu.VMEM((BLOCKS, PLANES, LANES), f32),
            pltpu.VMEM((2, SIDE, SLOTS, SIDE, PLANES, LANES), f32),
            pltpu.VMEM((oris, slice_columns), bf16),
            pltpu.VMEM((BATCHES, SIDE, CORES, SLOTS, SIDE, group, slice_columns), bf16),
            pltpu.VMEM((AHEAD, peers, CORES, SLOTS, group, half), bf16),
            pltpu.VMEM((AHEAD, peers, CORES, SLOTS, group, half), bf16),
            pltpu.VMEM((2, CORES, oris, lanes), f32),
            pltpu.VMEM((rounds, oris, lanes), f32),
            pltpu.VMEM((BATCHES, SIDE, oris, lanes), f32),
            pltpu.VMEM((BATCHES, 2, mid_ori, lanes), f32),
            pltpu.VMEM((BATCHES, peers, oris, lanes), f32),
            pltpu.VMEM((BATCHES, BLOCKS, 8, lanes), f32),
            pltpu.VMEM((BATCHES, SIDE, CORES, oris, lanes), bf16),
            pltpu.VMEM((BATCHES, SIDE, CORES, 8, lanes), f32),
            pltpu.VMEM((1, lanes), f32),
            pltpu.VMEM((oris, slice_columns), f32),
            dma((3,)),
            dma((PLANES - 1, 2)),
            dma((SIDE, CORES, 2)),
            dma((PLANES - 1,)),
            dma((SIDE, CORES)),
            dma((BLOCKS - 1,)),
            dma((BLOCKS - 1,)),
            dma((PLANES, 4)),
            dma((PLANES, 4)),
            dma((PLANES, 4)),
            dma((PLANES, 4)),
            dma((AHEAD, peers)),
            dma((rounds, peers)),
            dma((AHEAD, peers)),
            dma((rounds, peers)),
            dma((2,)),
            dma((rounds,)),
            dma((BATCHES, 2)),
            dma((BATCHES, 2)),
            dma((BATCHES, peers)),
            dma((BATCHES, peers)),
            dma((BATCHES, BLOCKS - 1)),
            dma((BATCHES, BLOCKS - 1)),
            dma((BATCHES, SIDE, 2)),
            dma((BATCHES, SIDE, 2)),
            dma((BATCHES, SIDE)),
            dma((BATCHES, SIDE)),
            dma((BATCHES, PLANES - 1)),
            dma((BATCHES, SIDE, CORES)),
        ],
        compiler_params=pltpu.CompilerParams(collective_id=0, has_side_effects=True, vmem_limit_bytes=62 * 2**20),
        cost_estimate=pl.CostEstimate(flops=15 * 10**9, bytes_accessed=32 * 2**20, transcendentals=10**6),
    )(search, images, projections)
    return weighted, loglik.reshape(-1)


def solution(mesh):
    placed = (P(("img", "ori"), None), P("ori", None), P(("img", "ori"), None))
    return jax.shard_map(
        per_device,
        mesh=mesh,
        in_specs=placed,
        out_specs=(P("ori", "img"), P(("img", "ori"))),
        check_vma=False,
    )
```

time: 167 us -> 152 us (0.910)
  Pallas kernels: 162 us -> 148 us
    pallas_call x1, Pallas kernels: 162 us -> 148 us  [per_device(): pl.pallas_call(kernel, out_shape=(jax.ShapeDtypeStruct((oris, slice_colum...]
where the time goes in v3:
time: 152 us
  Pallas kernels  148 us (97%)
  local copies, waits for them, and re-layouts  3.31 us (2%)
    pallas_call x1, Pallas kernels, per_device(): pl.pallas_call(kernel, out_shape=(jax.ShapeDtypeStruct((oris, slice_colum...  148 us
    unnamed x4, local copies, waits for them, and re-layouts  3.31 us

profile of v3, /device:TPU:1, one launch (start us, length us, event | category | flops | bytes accessed | tf_op | source)
XLA Modules:
  0.0 151.5 jit_solution(3355066935796749854)
XLA Ops:
  0.6 147.6 %shard_map.50 = (bf16[576,1536]{1,0:T(8,128)(2,1)}, f32[1,64]{1,0:T(1,128)}) custom-call(s32[4,4]{1,0:T(4,128)} %search.1, bf16[64,12288]{1,0:T(8,128)(2,1)} %images.1, bf16[576,12288]{1,0:T(8,128)(2,1)} %projections.1), custom_call_target="tpu_custom_call" | custom-call | flops 15000000512 | bytes 33554432 | tf_op jit(solution)/shard_map/pallas_call | solution.py:608
  148.2 0.0 copy-start
  148.2 2.8 %copy.7 = bf16[576,1536]{1,0:T(8,128)(2,1)} copy(bf16[576,1536]{1,0:T(8,128)(2,1)} %get-tuple-element.8) | data formatting | bytes 3538944
  151.0 0.0 copy-done
  151.0 0.5 copy.8
Async XLA Ops:
  148.2 2.8 %copy-start = (f32[1,64]{1,0:T(1,128)S(1)}, f32[1,64]{1,0:T(1,128)}, u32[]{:S(2)}) copy-start(f32[1,64]{1,0:T(1,128)} %get-tuple-element.5) | copy-start | bytes 772

commit v4 on v3

--- a/solution.py
+++ b/solution.py
@@ -17,7 +17,8 @@
 NO_SCORE = -3.0e38
 
 ROUNDS = [(2, 2), (1, 3), (3, 1), (0, 0)]
-ORDER = [(0, 3), (0, 1), (0, 2), (1, 3), (0, 0), (1, 0), (1, 1), (1, 2)] + [(q, r) for q in (2, 3) for r in range(4)]
+ORDER = [(0, 3), (0, 1), (0, 2), (1, 3), (0, 0), (1, 0), (1, 1), (1, 2)]
+ORDER += [(2, 0), (2, 1), (2, 2), (3, 0), (3, 1), (3, 2), (2, 3), (3, 3)]
 RELAYED = (1, 2, 3)
 
 
@@ -504,21 +505,21 @@
 
     tile = 2 * LANES
 
-    def add(q, ds):
-        for d in ds:
+    def add(parts, first=False, final=False):
+        for q, d in parts:
             crossed[q, d].wait_recv()
             for cc in range(CORES) if d else (other,):
                 ref = scale.at[q, d, cc]
                 remote(ref, ref, f_send.at[q, 0], f_recv.at[q, d, cc], partner).wait_recv()
-        first, final = q == 0, q == BATCHES - 1 and 2 in ds
-        pieces = [(d, cc) for d in ds for cc in range(CORES)]
+        pieces = [(q, d, cc) for q, d in parts for cc in range(CORES)]
         factor = jnp.concatenate(
-            [(resp[q, d, cc].astype(jnp.float32) * scale[q, d, cc, 0:1, :]).astype(jnp.bfloat16) for d, cc in pieces], axis=1
+            [(resp[q, d, cc].astype(jnp.float32) * scale[q, d, cc, 0:1, :]).astype(jnp.bfloat16) for q, d, cc in pieces],
+            axis=1,
         )
         for t in range(slice_columns // tile):
             cols = slice(t * tile, (t + 1) * tile)
             values = []
-            for d, cc in pieces:
+            for q, d, cc in pieces:
                 r = [pair[cc] for pair in ROUNDS].index(d)
                 values.append(arrived[q, r, cc, :, :, :, cols].reshape(lanes, tile))
             part = jnp.dot(factor, jnp.concatenate(values, axis=0), preferred_element_type=jnp.float32)
@@ -529,22 +530,22 @@
             else:
                 total[:, cols] = part
 
-    shares_at, passes_at = {8: 0, 11: 1, 15: 2}, {8: (6, 7), 11: (9, 10), 13: (13,), 14: (14,)}
+    passes_at = {7: (6,), 8: (7,), 10: (9,), 11: (10,), 12: (12,), 13: (13,)}
     for n in range(len(order)):
         for copy in moves[n]:
             copy.wait_recv()
-        if n in shares_at:
-            share(shares_at[n])
-            gather_near(shares_at[n])
+        if n == 8:
+            share(0)
+            gather_near(0)
         if n == 1:
             wait_far(6)
             wait_far(7)
         if n + AHEAD < len(order):
             refill(n)
         begin(n)
-        if 0 < n <= 12:
+        if 0 < n <= 11:
             finish(n - 1)
-        if n >= 12:
+        if n >= 11:
             finish(n)
         for k in passes_at.get(n, ()):
             pass_on(k)
@@ -552,29 +553,30 @@
             gather_far(0)
         if n == 10:
             respond(0)
+            share(1)
+            gather_near(1)
         if n == 11:
             gather_last(0)
         if n == 13:
-            add(0, range(SIDE))
             gather_far(1)
+            respond(1)
+            add([(0, d) for d in range(SIDE)], first=True)
         if n == 14:
-            respond(1)
-    gather_far(2)
+            share(2)
+            gather_near(2)
     share(3)
     gather_direct(3)
     gather_last(1)
-    add(1, range(SIDE))
+    add([(1, d) for d in range(SIDE)])
     respond(2)
-    gather_last(2)
+    gather_far(2)
     respond(3)
-    add(2, range(SIDE))
-    for d in (1, 3):
+    add([(2, 0), (2, 1), (2, 3), (3, 0)])
+    for d in (2, 1, 3):
         direct[3, d].wait_recv()
         cross(3, d)
-    add(3, (0, 1, 3))
-    direct[3, 2].wait_recv()
-    cross(3, 2)
-    add(3, (2,))
+    gather_last(2)
+    add([(3, 2), (3, 1), (3, 3), (2, 2)], final=True)
     loglik[...] = result[:, 0 : loglik.shape[1]]
 
     for copy in list(near.values()) + list(far.values()):

time: 152 us -> 147 us (0.967)
  Pallas kernels: 148 us -> 142 us
    pallas_call x1, Pallas kernels: 148 us -> 142 us  [per_device(): pl.pallas_call(kernel, out_shape=(jax.ShapeDtypeStruct((oris, slice_colum...]
where the time goes in v4:
time: 147 us; the launch traced here: 146 us
  Pallas kernels  142 us (97%)
  local copies, waits for them, and re-layouts  3.31 us (2%)
    pallas_call x1, Pallas kernels, per_device(): pl.pallas_call(kernel, out_shape=(jax.ShapeDtypeStruct((oris, slice_colum...  142 us
    unnamed x4, local copies, waits for them, and re-layouts  3.31 us

profile of v4, /device:TPU:1, one launch (start us, length us, event | category | flops | bytes accessed | tf_op | source)
XLA Modules:
  0.0 146.4 jit_solution(14408482247813729377)
XLA Ops:
  0.6 142.4 %shard_map.50 = (bf16[576,1536]{1,0:T(8,128)(2,1)}, f32[1,64]{1,0:T(1,128)}) custom-call(s32[4,4]{1,0:T(4,128)} %search.1, bf16[64,12288]{1,0:T(8,128)(2,1)} %images.1, bf16[576,12288]{1,0:T(8,128)(2,1)} %projections.1), custom_call_target="tpu_custom_call" | custom-call | flops 15000000512 | bytes 33554432 | tf_op jit(solution)/shard_map/pallas_call | solution.py:610
  143.1 0.0 copy-start
  143.1 2.8 %copy.7 = bf16[576,1536]{1,0:T(8,128)(2,1)} copy(bf16[576,1536]{1,0:T(8,128)(2,1)} %get-tuple-element.8) | data formatting | bytes 3538944
  145.9 0.0 copy-done
  145.9 0.5 copy.8
Async XLA Ops:
  143.1 2.8 %copy-start = (f32[1,64]{1,0:T(1,128)S(1)}, f32[1,64]{1,0:T(1,128)}, u32[]{:S(2)}) copy-start(f32[1,64]{1,0:T(1,128)} %get-tuple-element.5) | copy-start | bytes 772

commit v5 on v4

--- a/solution.py
+++ b/solution.py
@@ -479,14 +479,6 @@
                 )
                 direct[q, d, h].start()
 
-    def gather_direct(q):
-        cross(q, 0)
-        for d in (2, 1, 3):
-            direct[q, d] = remote(
-                resp.at[q, 0, c], resp.at[q, d, c], r_send.at[q, d, 0], r_recv.at[q, d, 0], at_img(ring(y, -d), c)
-            )
-            direct[q, d].start()
-
     def gather_far(q):
         for d, h in ((1, 0), (3, 1)):
             direct[q, d, h].wait_recv()
@@ -565,17 +557,16 @@
             share(2)
             gather_near(2)
     share(3)
-    gather_direct(3)
+    gather_near(3)
     gather_last(1)
     add([(1, d) for d in range(SIDE)])
     respond(2)
     gather_far(2)
     respond(3)
+    gather_far(3)
     add([(2, 0), (2, 1), (2, 3), (3, 0)])
-    for d in (2, 1, 3):
-        direct[3, d].wait_recv()
-        cross(3, d)
     gather_last(2)
+    gather_last(3)
     add([(3, 2), (3, 1), (3, 3), (2, 2)], final=True)
     loglik[...] = result[:, 0 : loglik.shape[1]]
 

time: 147 us -> 144 us (0.980)
  Pallas kernels: 142 us -> 140 us
    pallas_call x1, Pallas kernels: 142 us -> 140 us  [per_device(): pl.pallas_call(kernel, out_shape=(jax.ShapeDtypeStruct((oris, slice_colum...]
where the time goes in v5:
time: 144 us
  Pallas kernels  140 us (97%)
  local copies, waits for them, and re-layouts  3.31 us (2%)
    pallas_call x1, Pallas kernels, per_device(): pl.pallas_call(kernel, out_shape=(jax.ShapeDtypeStruct((oris, slice_colum...  140 us
    unnamed x4, local copies, waits for them, and re-layouts  3.31 us

profile of v5, /device:TPU:1, one launch (start us, length us, event | category | flops | bytes accessed | tf_op | source)
XLA Modules:
  0.0 143.8 jit_solution(2194911382806451133)
XLA Ops:
  0.6 139.8 %shard_map.50 = (bf16[576,1536]{1,0:T(8,128)(2,1)}, f32[1,64]{1,0:T(1,128)}) custom-call(s32[4,4]{1,0:T(4,128)} %search.1, bf16[64,12288]{1,0:T(8,128)(2,1)} %images.1, bf16[576,12288]{1,0:T(8,128)(2,1)} %projections.1), custom_call_target="tpu_custom_call" | custom-call | flops 15000000512 | bytes 33554432 | tf_op jit(solution)/shard_map/pallas_call | solution.py:601
  140.4 0.0 copy-start
  140.5 2.8 %copy.7 = bf16[576,1536]{1,0:T(8,128)(2,1)} copy(bf16[576,1536]{1,0:T(8,128)(2,1)} %get-tuple-element.8) | data formatting | bytes 3538944
  143.3 0.0 copy-done
  143.3 0.5 copy.8
Async XLA Ops:
  140.4 2.8 %copy-start = (f32[1,64]{1,0:T(1,128)S(1)}, f32[1,64]{1,0:T(1,128)}, u32[]{:S(2)}) copy-start(f32[1,64]{1,0:T(1,128)} %get-tuple-element.5) | copy-start | bytes 772
